TPU v7x, 512 devices: a whole 4x4x16 slice. The times are simulated.
512 devices in a mesh: member: 8 (over z_lo, core), space: 64 (over x, z_hi, y).
Axes of the slice: x: 4, y: 4, z: 16 (z_hi: 4, z_lo: 4; z = z_hi * 4 + z_lo), core: 2. Of those that a mesh axis runs over, the one named last changes fastest.
Arguments:
- hidden: bfloat16 [8, 49152, 1024], P('member', 'space'), may hold values from -16 to 16
- truth: float32 [100, 49152], P(None, 'space'), may hold values from -6 to 6
- lat_row: int32 [49152], P('space'), may hold values from 0 to 720
- gain: float32 [1024], replicated, may hold values from 0.25 to 1.75
- w_in: bfloat16 [1024, 1024], P('space'), may hold values from -0.1875 to 0.1875
- w_out: bfloat16 [100, 1024], replicated, may hold values from -0.1875 to 0.1875
Outputs:
- grad_hidden: bfloat16 [8, 49152, 1024], P('member', 'space')
- grad_w1: float32 [1024, 1024], P('space')
Inputs may be any that keep to these rules, and one draw needn't show every extreme that they name: `lat_row`: global latitude row of each grid point.
All inputs are finite; a program needn't handle non-finite values.
Results may differ from a plain program's by a relative error of at most 0.012.
Values may be sent and summed in bfloat16 or wider, within the bound.
A program may use at most 64 MiB of HBM per device.

v0:
```python
import math

import jax
import jax.numpy as jnp
from jax import lax
from jax.sharding import PartitionSpec as P

LATS = 721


ALPHA = 0.95
SMOOTH = 0.1
LOSS_SCALE = 64.0
EPSILON = 1e-05


def slope(diff):
    return diff / jnp.sqrt(diff * diff + SMOOTH * SMOOTH)


def per_device(hidden, truth, lat_row, gain, w_in, w_out):
    count = lax.axis_size("member")
    spaces = lax.axis_size("space")
    local_points = hidden.shape[1]
    rows = hidden[0].astype(jnp.float32)
    root_mean = jnp.sqrt(jnp.mean(rows * rows, axis=-1, keepdims=True) + EPSILON)
    unit_rows = rows / root_mean
    normed = (unit_rows * gain).astype(jnp.bfloat16)
    full_first = lax.all_gather(w_in, "space", axis=0, tiled=True)
    preact = jnp.dot(normed, full_first, preferred_element_type=jnp.float32)
    hidden_act = jax.nn.silu(preact).astype(jnp.bfloat16)
    fields = lax.dot_general(
        w_out, hidden_act, (((1,), (1,)), ((), ())), preferred_element_type=jnp.float32
    )
    coarse = lax.optimization_barrier(fields.astype(jnp.bfloat16))
    own_coarse = coarse.astype(jnp.float32)
    everyone = lax.all_gather(coarse[None], "member", axis=0, tiled=True)
    pairs = jnp.sum(slope(own_coarse[None] - everyone.astype(jnp.float32)), axis=0)
    latitude = math.pi * ((lat_row.astype(jnp.float32) + 0.5) / LATS - 0.5)
    area = jnp.cos(latitude)[None, :]
    fair = (1.0 - (1.0 - ALPHA) / count) / (count * (count - 1))
    grad_fields = (LOSS_SCALE * area * (slope(fields - truth) / count - fair * pairs)).astype(
        jnp.bfloat16
    )
    grad_act = lax.dot_general(
        grad_fields, w_out, (((0,), (0,)), ((), ())), preferred_element_type=jnp.float32
    )
    sigma = jax.nn.sigmoid(preact)
    grad_pre = (grad_act * sigma * (1.0 + preact * (1.0 - sigma))).astype(jnp.bfloat16)
    grad_normed = lax.dot_general(
        grad_pre, full_first, (((1,), (1,)), ((), ())), preferred_element_type=jnp.float32
    )
    scaled = grad_normed * gain
    inner = jnp.mean(scaled * unit_rows, axis=-1, keepdims=True)
    grad_rows = ((scaled - unit_rows * inner) / root_mean).astype(jnp.bfloat16)
    owned = lax.psum_scatter(
        lax.dot_general(
            normed, grad_pre, (((0,), (0,)), ((), ())), preferred_element_type=jnp.float32
        ),
        "space",
        scatter_dimension=0,
        tiled=True,
    )
    owned = lax.psum(owned.astype(jnp.bfloat16), "member").astype(jnp.float32)
    factor = 1.0 / math.sqrt(count * local_points * spaces)
    return (grad_rows[None], owned * factor)


def solution(mesh):
    in_specs = (
        P("member", "space", None),
        P(None, "space"),
        P("space"),
        P(),
        P("space", None),
        P(),
    )
    out_specs = (P("member", "space", None), P("space", None))
    return jax.shard_map(
        per_device, mesh=mesh, in_specs=in_specs, out_specs=out_specs, check_vma=False
    )
```

profile of v0, /device:TPU:1, one launch (start us, length us, event | category | flops | bytes accessed | tf_op | source)
XLA Modules:
  0.0 675.7 jit_solution(11655391293714292702)
XLA Ops:
  7.2 0.0 copy-start
  7.2 0.0 all-gather.5.cloned.1.call-start
  7.2 0.7 all-gather.5.cloned.1.call-update
  7.9 0.0 all-gather.7.cloned.1.call-start
  8.0 1.8 fusion
  9.8 120.7 %all-gather.5.cloned.1.call-done = bf16[1024,1024]{1,0:T(8,128)(2,1)} async-done(((bf16[16,1024]{1,0:T(8,128)(2,1)}), bf16[1024,1024]{1,0:T(8,128)(2,1)}) %all-gather.5.cloned.1.call-update) | async-done | bytes 2097168 | tf_op jit(solution)/shard_map/all_gather | solution.py:29
  130.5 3.9 fusion.10
  134.4 0.0 copy-done
  134.4 0.0 copy-start.2
  134.4 0.0 copy-start.4
  134.5 1.7 fusion.19
  136.1 0.0 copy-done.5
  136.1 0.0 all-gather.7.cloned.1.call-update
  136.2 0.0 reduce-scatter.2.cloned.1.call-start
  136.3 0.9 convert_element_type.45
  137.2 36.0 %all-gather.7.cloned.1.call-done = bf16[8,100,768]{2,1,0:T(8,128)(2,1)} async-done(((bf16[1,100,768]{2,1,0:T(8,128)(2,1)}), bf16[8,100,768]{2,1,0:T(8,128)(2,1)}) %all-gather.7.cloned.1.call-update) | async-done | bytes 1228816 | tf_op jit(solution)/shard_map/all_gather | solution.py:37
  173.2 1.9 fusion.5
  175.1 0.0 copy-done.4
  175.1 0.0 copy-start.1
  175.2 0.0 copy-start.3
  175.2 3.4 multiply_convert_fusion
  178.5 0.0 copy-start.6
  178.6 1.1 copy-done.6
  179.7 0.0 copy-done.3
  179.7 4.0 fusion.9
  183.7 0.0 reduce-scatter.2.cloned.1.call-update
  183.7 4.1 multiply_reduce_fusion
  187.9 2.0 fusion.7
  189.9 406.4 %reduce-scatter.2.cloned.1.call-done = f32[16,1024]{1,0:T(8,128)} async-done(((f32[1024,1024]{1,0:T(8,128)}), f32[16,1024]{1,0:T(8,128)}) %reduce-scatter.2.cloned.1.call-update) | async-done | bytes 65552 | tf_op jit(solution)/shard_map/reduce_scatter | solution.py:56
  596.2 0.8 convert_element_type.50
  597.1 71.5 %psum.7 = bf16[16,1024]{1,0:T(8,128)(2,1)S(1)} all-reduce(bf16[16,1024]{1,0:T(8,128)(2,1)S(1)} %convert_element_type.50), channel_id=1, replica_groups=mesh['member'=8,'space'=64] {'member'}, use_global_device_ids=true, to_apply=%region_4.5 | all-reduce | flops 16384 | bytes 65536 | tf_op jit(solution)/shard_map/psum | solution.py:64
  668.5 0.6 convert_multiply_fusion.1
  (6 shorter events, 0.1 us)
Async XLA Ops:
  7.2 127.2 %copy-start = (bf16[100,1024]{1,0:T(8,128)(2,1)S(1)}, bf16[100,1024]{1,0:T(8,128)(2,1)}, u32[]{:S(2)}) copy-start(bf16[100,1024]{1,0:T(8,128)(2,1)} %param.11) | copy-start | bytes 614404
  7.2 123.3 %all-gather.5.cloned.1.call-start = ((), (), s32[]{:S(2)}) async-start(), calls=%async_computation.1 | async-start | bytes 2129920 | tf_op jit(solution)/shard_map/all_gather | solution.py:29
  7.9 165.3 %all-gather.7.cloned.1.call-start = ((), (), s32[]{:S(2)}) async-start(), calls=%async_computation.3 | async-start | bytes 1437696 | tf_op jit(solution)/shard_map/all_gather | solution.py:37
  134.4 1.7 copy-start.5
  134.4 1.8 copy-start.2
  134.4 40.7 %copy-start.4 = (f32[100,768]{1,0:T(8,128)S(1)}, f32[100,768]{1,0:T(8,128)}, u32[]{:S(2)}) copy-start(f32[100,768]{1,0:T(8,128)} %param.7) | copy-start | bytes 921604
  136.2 460.1 %reduce-scatter.2.cloned.1.call-start = ((), (), s32[]{:S(2)}) async-start(), calls=%async_computation.2 | async-start | bytes 4259840 | tf_op jit(solution)/shard_map/reduce_scatter | solution.py:56
  175.1 4.5 copy-start.1
  175.2 4.5 copy-start.3
  178.5 1.1 copy-start.6
Sparse Core Ops, SparseCore 0:
  12.2 118.2 all-gather.4
  136.3 36.8 all-gather.6
  183.9 412.3 reduce-scatter.1
where the time goes:
time: 676 us
  waiting for transfers between devices  564 us (83%)
  blocking collectives  71.5 us (11%)
  matrix products  17.1 us (3%)
  between operations  13.9 us (2%)
  other arithmetic  8.18 us (1%)
    reduce_scatter x1, waiting for transfers between devices, per_device(): lax.psum_scatter(lax.dot_general(normed, grad_pre, (((0,), (0,)), ((), ()...  406 us
    all_gather x1, waiting for transfers between devices, per_device(): full_first = lax.all_gather(w_in, 'space', axis=0, tiled=True)  121 us
    psum x1, blocking collectives, per_device(): owned = lax.psum(owned.astype(jnp.bfloat16), 'member').astype(jnp.float32)  71.5 us
    all_gather x1, waiting for transfers between devices, per_device(): everyone = lax.all_gather(coarse[None], 'member', axis=0, tiled=True)  36 us
  transfers between devices with their start and end apart: 3, of which 3 were waited for; matrix products, arithmetic and copies ran while one was open for 1% of the time, Pallas kernels for 0%

commit v1 on v0

v1 whole, which is shorter than its diff:
```python
import functools
import math

import jax
import jax.numpy as jnp
from jax import lax
from jax.experimental import pallas as pl
from jax.experimental.pallas import tpu as pltpu
from jax.sharding import PartitionSpec as P

LATS = 721
ALPHA = 0.95
SMOOTH = 0.1
LOSS_SCALE = 64.0
EPSILON = 1e-05

GRID = (4, 4, 4)
LANES = 128
TILE = 256
MESH = pl.DeviceIdType.MESH


def slope(diff):
    return diff * lax.rsqrt(diff * diff + SMOOTH * SMOOTH)


def rows_at(start, size):
    return pl.ds(pl.multiple_of(start, size), size)


def kernel(
    tile,
    hid_hbm, truth_hbm, lat_hbm, gain_hbm, w_hbm, wo_hbm,
    gh, gw_ref,
    hid, truth, lat, gain, wo_raw, w_full, normed, planes, inv_root, wo_pad, wo_t, hidden_act,
    truth_pad, truth_t, area_t, act, fields, coarse, theirs, answers, pairs, gp,
    csend, crecv, sums, send1, recv1, send2, recv2, send3, recv3, finals,
    local_sem, a1_s, a1_r, a2_s, a2_r, a3_s, a3_r, a4_s, a4_r,
    b1_s, b1_r, b2_s, b2_r, c0_s, c0_r, c1_s, c1_r, c2_s, c2_r, c3_s, c3_r, c4_s, c4_r,
):
    nx, nh, ny = GRID
    n = nx
    points, width = hid.shape
    half = width // 2
    quarter = half // 2
    levels = truth.shape[0]
    count = finals.shape[0]
    chips = count // 2
    block = w_full.shape[3]
    tiles, share = theirs.shape[0], theirs.shape[2]
    f32, bf16 = jnp.float32, jnp.bfloat16

    member, space = lax.axis_index("member"), lax.axis_index("space")
    core, low = member % 2, member // 2
    x, h, y = space // (nh * ny), (space // ny) % nh, space % ny
    q, p = x * (1 - core) + y * core, y * (1 - core) + x * core
    mine = pl.ds(pl.multiple_of(core * half, half), half)
    other = pl.ds(pl.multiple_of((1 - core) * half, half), half)
    quarters = [
        pl.ds(pl.multiple_of(core * half + i * quarter, quarter), quarter) for i in range(2)
    ]

    def place(p_, q_):
        return q_ * (1 - core) + p_ * core, p_ * (1 - core) + q_ * core

    def at(p_, q_, h_):
        x_, y_ = place(p_, q_)
        return (member, (x_ * nh + h_) * ny + y_)

    def h_peer(k):
        return at(p, q, (h + k) % nh)

    def q_peer(k):
        return at(p, (q + k) % n, h)

    def m_peer(k):
        return ((member + k) % count, space)

    def z_peer(i):
        dh, dl = i // chips, i % chips
        return (2 * ((low + dl) % chips) + core, (x * nh + (h + dh) % nh) * ny + y)

    sides = [p + 1 - 2 * (p % 2), n - 1 - p]
    far = (p + 2) % n
    p_peers = [at(v, q, h) for v in sides]
    partner = (member + 1 - 2 * core, space)

    def send(src, dst, send_sem, recv_sem, target):
        pltpu.make_async_remote_copy(
            src_ref=src, dst_ref=dst, send_sem=send_sem, recv_sem=recv_sem,
            device_id=target, device_id_type=MESH,
        ).start()

    def drain(ref, sem):
        pltpu.make_async_copy(ref, ref, sem).wait()

    def loop(first, last, body):
        def step(i, carry):
            body(i)
            return carry

        lax.fori_loop(first, last, step, 0)

    barrier = pltpu.get_barrier_semaphore()

    def greet(peer):
        pl.semaphore_signal(barrier, inc=1, device_id=peer, device_id_type=MESH)

    loop(chips, nh * chips, lambda i: greet(z_peer(i)))
    loop(1, n, lambda k: greet(q_peer(k)))
    for peer in p_peers:
        greet(peer)
    loop(1, count, lambda k: greet(m_peer(k)))

    own_w = pltpu.make_async_copy(w_hbm.at[:, mine], w_full.at[x, h, y, :, mine], local_sem.at[0])
    loads = [
        pltpu.make_async_copy(source, target, local_sem.at[1 + i])
        for i, (source, target) in enumerate(
            [(hid_hbm, hid), (gain_hbm, gain), (truth_hbm, truth), (lat_hbm, lat), (wo_hbm, wo_raw)]
        )
    ]
    own_w.start()
    for load in loads:
        load.start()
    pl.semaphore_wait(barrier, nh * chips - chips + n - 1 + 2 + count - 1)

    own_block = w_full.at[x, h, y, :, mine]
    loop(1, nh, lambda k: send(w_hbm.at[:, mine], own_block, a1_s.at[0], a1_r.at[0], h_peer(k)))
    loads[0].wait()
    loads[1].wait()

    def normalise(i):
        rows = rows_at(i * 32, 32)
        values = hid[rows, :].astype(f32)
        root = jnp.sqrt(jnp.mean(values * values, axis=-1, keepdims=True) + EPSILON)
        inverse = 1.0 / root
        inv_root[rows, :] = jnp.broadcast_to(inverse, (32, LANES))
        normed[rows, :] = (values * inverse * gain[...]).astype(bf16)

    steps = points // 32
    loop(0, steps, normalise)
    own_w.wait()
    z_blocks = w_full.at[0, 0, pl.ds(0, nh - 1), :, mine]
    drain(z_blocks, a1_r.at[0])

    def group(p_, b, cols=mine):
        x_, y_ = place(p_, (q - b + n) % n)
        return w_full.at[x_, :, y_, :, cols]

    def to_partner(p_, b):
        part = group(p_, b)
        send(part, part, a4_s.at[0], a4_r.at[0], partner)

    def to_second(b):
        part = group(p, b)
        for i in range(2):
            send(part, part, a3_s.at[0], a3_r.at[b, i], p_peers[i])
        to_partner(p, b)

    def ordered(j):
        return j + (j // 2) * (n + 1 - 2 * j)

    own_group = group(p, 0)
    loop(1, n, lambda j: send(
        own_group, own_group, a2_s.at[0], a2_r.at[ordered(j) - 1], q_peer(ordered(j))
    ))
    to_second(0)
    for load in loads[2:]:
        load.wait()
    truth_pad[...] = jnp.zeros_like(truth_pad)
    truth_pad[0:levels, :] = truth[...]
    wo_pad[...] = jnp.zeros_like(wo_pad)
    wo_pad[0:levels, :] = wo_raw[...]

    def pass_first(j):
        b = ordered(j)
        drain(own_group, a2_r.at[b - 1])
        to_second(b)

    loop(1, n, pass_first)

    def pass_second(j):
        b = ordered(j)
        for i in range(2):
            drain(own_group, a3_r.at[b, i])
            part = group(sides[i], b, quarters[i])
            send(part, part, a3_s.at[0], a3_r.at[b, 2 + i], p_peers[1 - i])
        for i in range(2):
            to_partner(sides[i], b)

    loop(0, n, pass_second)

    def pass_far(j):
        b = ordered(j)
        for i in range(2):
            drain(group(far, b, quarters[i]), a3_r.at[b, 2 + i])
        to_partner(far, b)

    loop(0, n, pass_far)

    def project(rows, cols):
        act[rows, cols] = jnp.dot(
            normed[rows, :], w_full[:, :, :, :, cols].reshape(width, half),
            preferred_element_type=f32,
        )

    def activate(i, cols):
        rows = rows_at(i * 32, 32)
        a = act[rows, cols]
        hidden_act[rows, cols] = (a * (0.5 * jnp.tanh(0.5 * a) + 0.5)).astype(bf16)

    loop(0, tiles, lambda t: project(rows_at(t * tile, tile), mine))
    loop(0, steps, lambda i: activate(i, mine))

    truth_t[...] = truth_pad[...].T
    latitude = math.pi * ((lat[...].astype(f32) + 0.5) / LATS - 0.5)
    area = LOSS_SCALE * jnp.cos(latitude)
    strip = lat.shape[1]
    for i in range(lat.shape[0]):
        area_t[i * strip:(i + 1) * strip, :] = jnp.broadcast_to(area[i:i + 1, :], (LANES, strip)).T
    wo_t[...] = wo_pad[...].T
    drain(w_full.at[:, :, :, :, other], a4_r.at[0])

    def share_of(t, m):
        return rows_at(t * tile + m * share, share)

    tile_steps = tile // 32

    def forward(t):
        rows = rows_at(t * tile, tile)
        project(rows, other)
        loop(t * tile_steps, (t + 1) * tile_steps, lambda i: activate(i, other))
        field = jnp.dot(hidden_act[rows, :], wo_t[...], preferred_element_type=f32)
        fields[rows, :] = field
        coarse[rows, :] = field.astype(bf16)

        def spread(k):
            peer = m_peer(k)
            send(
                coarse.at[share_of(t, peer[0]), :], theirs.at[t, member],
                b1_s.at[0], b1_r.at[t], peer,
            )

        loop(1, count, spread)
        theirs[t, member] = coarse[share_of(t, member), :]

    loop(0, tiles, forward)

    def differentiate(i):
        rows = rows_at(i * 32, 32)
        a = act[rows, :]
        s = 0.5 * jnp.tanh(0.5 * a) + 0.5
        act[rows, :] = s * (1.0 + a * (1.0 - s))

    span = min(LANES, points)
    turns = points // span

    def turn(i):
        cols = rows_at(i * span, span)
        turned = normed[cols, :].T
        for x_ in range(nx):
            for h_ in range(nh):
                for y_ in range(ny):
                    first = ((x_ * nh + h_) * ny + y_) * block
                    piece = turned[first:first + block, :]
                    to_x, to_y = (x_ * nh + h_) * block, (y_ * nh + h_) * block
                    planes[0, y_, to_x:to_x + block, cols] = piece
                    planes[1, x_, to_y:to_y + block, cols] = piece

    def answer(t):
        come = theirs.at[t, pl.ds(0, count - 1)]
        drain(come, b1_r.at[t])

        def compare(i):
            rows = rows_at(i * 16, 16)
            values = [theirs[t, m, rows, :].astype(f32) for m in range(count)]
            totals = [jnp.zeros_like(values[0]) for m in range(count)]
            for m in range(count):
                for o in range(m + 1, count):
                    s = slope(values[m] - values[o])
                    totals[m] = totals[m] + s
                    totals[o] = totals[o] - s
            for m in range(count):
                answers[t, m, rows, :] = totals[m].astype(bf16)

        loop(0, share // 16, compare)

        def reply(k):
            peer = m_peer(k)
            send(
                answers.at[t, peer[0]], pairs.at[share_of(t, member), :],
                b2_s.at[0], b2_r.at[t], peer,
            )

        loop(1, count, reply)
        pairs[share_of(t, member), :] = answers[t, member]
        loop(t * tile_steps, (t + 1) * tile_steps, differentiate)
        loop(t * turns // tiles, (t + 1) * turns // tiles, turn)

    loop(0, tiles, answer)

    fair = (1.0 - (1.0 - ALPHA) / count) / (count * (count - 1))

    def backward(t):
        come = pairs.at[pl.ds(0, tile - share), :]
        drain(come, b2_r.at[t])
        rows = rows_at(t * tile, tile)
        grad_fields = area_t[rows, :] * (
            slope(fields[rows, :] - truth_t[rows, :]) * (1.0 / count)
            - fair * pairs[rows, :].astype(f32)
        )
        grad_act = jnp.dot(grad_fields.astype(bf16), wo_pad[...], preferred_element_type=f32)
        gp[rows, :] = (grad_act * act[rows, :]).astype(bf16)

    loop(0, tiles, backward)

    depth = width // n

    def nth(i, own):
        first = jnp.where(i == 0, (own + 2) % n, own + 1 - 2 * (own % 2))
        return jnp.where(i < 2, first, jnp.where(i == 2, n - 1 - own, own))

    def other_plane(i):
        part = jnp.dot(planes[1 - core, nth(i, q)], gp[:, other], preferred_element_type=f32)
        csend[i] = part.astype(bf16)
        send(csend.at[i], crecv.at[i], c0_s.at[0], c0_r.at[i], partner)

    loop(0, n, other_plane)

    halves = [slice(0, quarter), slice(quarter, half)]

    def to_side(slot, target):
        send(send1.at[slot], recv1.at[slot], c1_s.at[0], c1_r.at[slot], p_peers[target])

    def own_plane(i):
        part = jnp.dot(planes[core, nth(i, p)], gp[:, mine], preferred_element_type=f32)
        drain(crecv.at[i], c0_r.at[i])
        total = part + crecv[i].astype(f32)
        sums[i] = total

        @pl.when(i == 0)
        def _():
            for side in range(2):
                send1[side] = total[:, halves[side]].astype(bf16)
                to_side(side, side)

        for side in range(2):
            @pl.when(i == 1 + side)
            def _():
                send1[2 + side] = total[:, halves[side]].astype(bf16)
                to_side(2 + side, side)

    loop(0, n, own_plane)
    for side in range(2):
        drain(recv1.at[side], c1_r.at[side])
        term = sums[2 - side, :, halves[side]] + recv1[side].astype(f32)
        send1[4 + side] = term.astype(bf16)
        to_side(4 + side, 1 - side)

    def grad_normed(x_):
        cols = rows_at(x_ * depth, depth)
        act[:, cols] = lax.dot_general(
            gp[...], w_full[x_].reshape(depth, width), (((1,), (1,)), ((), ())),
            preferred_element_type=f32,
        )

    def hidden_grad(i):
        rows = rows_at(i * 32, 32)
        scaled = act[rows, :] * gain[...]
        inverse = inv_root[rows, 0:1]
        unit = hid[rows, :].astype(f32) * inverse
        inner = jnp.mean(scaled * unit, axis=-1, keepdims=True)
        gh[rows, :] = ((scaled - unit * inner) * inverse).astype(bf16)

    loop(0, n // 2, grad_normed)
    for slot in range(2, 6):
        drain(recv1.at[slot], c1_r.at[slot])
    line_rows = nh * block

    def add_planes(q_):
        rows = rows_at(q_ * line_rows, line_rows)
        both = [
            sums[n - 1, rows, halves[i]] + recv1[2 + i, rows, :].astype(f32)
            + recv1[4 + i, rows, :].astype(f32)
            for i in range(2)
        ]
        return jnp.concatenate(both, axis=1)

    def to_first(j):
        k = ordered(n - j)
        send2[j - 1] = add_planes((q + k) % n).astype(bf16)
        send(send2.at[j - 1], recv2.at[j - 1], c2_s.at[0], c2_r.at[0], q_peer(k))

    loop(1, n, to_first)
    total = add_planes(q)
    loop(n // 2, n, grad_normed)
    drain(recv2, c2_r.at[0])
    for i in range(n - 1):
        total = total + recv2[i].astype(f32)
    strip = half // chips
    for h_ in range(nh):
        for l_ in range(chips):
            send3[h_, l_] = total[
                h_ * block:(h_ + 1) * block, l_ * strip:(l_ + 1) * strip
            ].astype(bf16)
    loop(1, nh * chips, lambda i: send(
        send3.at[(h + i // chips) % nh, (low + i % chips) % chips], recv3.at[i - 1],
        c3_s.at[0], c3_r.at[0], z_peer(i),
    ))
    loop(0, steps // 2, hidden_grad)
    drain(recv3, c3_r.at[0])
    total = send3[h, low].astype(f32)
    for i in range(nh * chips - 1):
        total = total + recv3[i].astype(f32)
    factor = 1.0 / math.sqrt(count * points * nx * nh * ny)
    finals[core * chips + low] = total * factor
    own_final = finals.at[core * chips + low]
    loop(1, count, lambda k: send(own_final, own_final, c4_s.at[0], c4_r.at[0], m_peer(k)))
    loop(steps // 2, steps, hidden_grad)
    others = finals.at[pl.ds(0, count - 1)]
    drain(others, c4_r.at[0])
    for i in range(count):
        gw_ref[:, i * strip:(i + 1) * strip] = finals[i]

    drain(z_blocks, a1_s.at[0])
    drain(w_full.at[pl.ds(0, n - 1), :, 0, :, mine], a2_s.at[0])
    drain(w_full.at[:, :, pl.ds(0, 3), :, mine], a3_s.at[0])
    drain(w_full.at[:, :, :, :, mine], a4_s.at[0])
    drain(coarse.at[pl.ds(0, points - points // count), :], b1_s.at[0])
    drain(coarse.at[pl.ds(0, points - points // count), :], b2_s.at[0])
    drain(csend, c0_s.at[0])
    drain(send1, c1_s.at[0])
    drain(send2, c2_s.at[0])
    drain(recv3, c3_s.at[0])
    drain(others, c4_s.at[0])


def hand_over(*arrays):
    pieces = 4

    def body(*refs):
        sources, targets, sems = refs[:len(arrays)], refs[len(arrays):-1], refs[-1]
        copies = []
        for source, target in zip(sources, targets):
            rows = source.shape[0]
            parts = pieces if rows % (16 * pieces) == 0 else 1
            for i in range(parts):
                part = pl.ds(i * (rows // parts), rows // parts)
                copies.append(
                    pltpu.make_async_copy(source.at[part], target.at[part], sems.at[len(copies)])
                )
        for copy in copies:
            copy.start()
        for copy in copies:
            copy.wait()

    anywhere = pl.BlockSpec(memory_space=pl.ANY)
    return pl.pallas_call(
        body,
        out_shape=tuple(jax.ShapeDtypeStruct(a.shape, a.dtype) for a in arrays),
        in_specs=[anywhere] * len(arrays),
        out_specs=(anywhere,) * len(arrays),
        scratch_shapes=[pltpu.SemaphoreType.DMA((pieces * len(arrays),))],
        compiler_params=pltpu.CompilerParams(vmem_limit_bytes=1024 * 1024),
        name="hand_over",
    )(*arrays)


def per_device(hidden, truth, lat_row, gain, w_in, w_out):
    nx, nh, ny = GRID
    count = lax.axis_size("member")
    _, points, width = hidden.shape
    levels = truth.shape[0]
    block = w_in.shape[0]
    half = width // 2
    tile = min(TILE, points)
    tiles, share = points // tile, tile // count
    f32, bf16 = jnp.float32, jnp.bfloat16
    vmem, dma = pltpu.VMEM, pltpu.SemaphoreType.DMA
    n, chips, lat_strip = nx, count // 2, min(LANES, points)
    scratch = [
        vmem((points, width), bf16),
        vmem((levels, points), f32),
        vmem((points // lat_strip, lat_strip), jnp.int32),
        vmem((1, width), f32),
        vmem((levels, width), bf16),
        vmem((nx, nh, ny, block, width), bf16),
        vmem((points, width), bf16),
        vmem((2, n, width // n, points), bf16),
        vmem((points, LANES), f32),
        vmem((LANES, width), bf16),
        vmem((width, LANES), bf16),
        vmem((points, width), bf16),
        vmem((LANES, points), f32),
        vmem((points, LANES), f32),
        vmem((points, LANES), f32),
        vmem((points, width), f32),
        vmem((points, LANES), f32),
        vmem((points, LANES), bf16),
        vmem((tiles, count, share, LANES), bf16),
        vmem((tiles, count, share, LANES), bf16),
        vmem((points, LANES), bf16),
        vmem((points, width), bf16),
        vmem((n, width // n, half), bf16),
        vmem((n, width // n, half), bf16),
        vmem((n, width // n, half), f32),
        vmem((6, width // n, half // 2), bf16),
        vmem((6, width // n, half // 2), bf16),
        vmem((n - 1, nh * block, half), bf16),
        vmem((n - 1, nh * block, half), bf16),
        vmem((nh, chips, block, half // chips), bf16),
        vmem((nh * chips - 1, block, half // chips), bf16),
        vmem((count, block, half // chips), f32),
        dma((6,)),
    ]
    for arrivals in (
        (1,), (n - 1,), (n, 4), (1,),
        (tiles,), (tiles,),
        (n,), (6,), (1,), (1,), (1,),
    ):
        scratch += [dma((1,)), dma(arrivals)]
    grad_rows, grad_first = pl.pallas_call(
        functools.partial(kernel, tile),
        out_shape=(
            vmem((points, width), bf16),
            vmem((block, width), f32),
        ),
        in_specs=[pl.BlockSpec(memory_space=pltpu.HBM)] * 6,
        out_specs=(pl.BlockSpec(memory_space=vmem),) * 2,
        scratch_shapes=scratch,
        compiler_params=pltpu.CompilerParams(
            collective_id=0, has_side_effects=True, vmem_limit_bytes=57 * 1024 * 1024
        ),
        name="crps_step",
    )(
        hidden[0], truth, lat_row.reshape(points // lat_strip, lat_strip), gain[None], w_in, w_out
    )
    grad_rows, grad_first = hand_over(grad_rows, grad_first)
    return (grad_rows[None], grad_first)


def solution(mesh):
    in_specs = (
        P("member", "space", None),
        P(None, "space"),
        P("space"),
        P(),
        P("space", None),
        P(),
    )
    out_specs = (P("member", "space", None), P("space", None))
    return jax.shard_map(
        per_device, mesh=mesh, in_specs=in_specs, out_specs=out_specs, check_vma=False
    )
```

time: 676 us -> 80.7 us (0.12)
  waiting for transfers between devices: 564 us -> 0 us
  Pallas kernels: 0 us -> 79.9 us
  blocking collectives: 71.5 us -> 0 us
  matrix products: 17.1 us -> 0 us
  between operations: 13.9 us -> 0.64 us
  other arithmetic: 8.18 us -> 0 us
    reduce_scatter x1 -> x0, waiting for transfers between devices: 406 us -> none  [per_device(): lax.psum_scatter(lax.dot_general(normed, grad_pre, (((0,), (0,)), ((), ()...]
    all_gather x2 -> x0, waiting for transfers between devices: 157 us -> none  [the longest x1 121 us: per_device(): full_first = lax.all_gather(w_in, 'space', axis=0, tiled=True)]
    pallas_call x0 -> x2, Pallas kernels: none -> 79.9 us  [the longest x1 78.7 us: per_device(): pl.pallas_call(functools.partial(kernel, tile), out_shape=(vmem((points,...]
    psum x1 -> x0, blocking collectives: 71.5 us -> none  [per_device(): owned = lax.psum(owned.astype(jnp.bfloat16), 'member').astype(jnp.float32)]
    dot_general x5 -> x0, matrix products: 17.1 us -> none  [the longest x1 4.1 us: per_device(): lax.dot_general(grad_pre, full_first, (((1,), (1,)), ((), ())), preferred...]
  transfers between devices with their start and end apart: 3 -> 0, of which waited for: 3 -> 0; matrix products, arithmetic and copies ran while one was open for 1% -> 0% of each run, Pallas kernels for 0% -> 0%
where the time goes in v1:
time: 80.7 us; the launch traced here: 80.6 us
  Pallas kernels  79.9 us (99%)
    pallas_call x1, Pallas kernels, per_device(): pl.pallas_call(functools.partial(kernel, tile), out_shape=(vmem((points,...  78.7 us

profile of v1, /device:TPU:1, one launch (start us, length us, event | category | flops | bytes accessed | tf_op | source)
XLA Modules:
  0.0 80.6 jit_solution(14232083147281072657)
XLA Ops:
  0.6 78.7 %crps_step.1 = (bf16[768,1024]{1,0:T(8,128)(2,1)S(1)}, f32[16,1024]{1,0:T(8,128)S(1)}) custom-call(bf16[768,1024]{1,0:T(8,128)(2,1)} %bitcast.4, f32[100,768]{1,0:T(8,128)} %truth_hbm.1, s32[6,128]{1,0:T(8,128)} %bitcast.5, f32[1,1024]{1,0:T(1,128)} %bitcast.6, bf16[16,1024]{1,0:T(8,128)(2,1)} %w_hbm.1, bf16[100,1024]{1,0:T(8,128)(2,1)} %wo_hbm.1), custom_call_target="tpu_custom_call" | custom-call | tf_op jit(solution)/shard_map/crps_step/pallas_call | solution.py:522
  79.4 1.2 %hand_over.1 = (bf16[768,1024]{1,0:T(8,128)(2,1)}, f32[16,1024]{1,0:T(8,128)}) custom-call(bf16[768,1024]{1,0:T(8,128)(2,1)S(1)} %get-tuple-element.6.refs_0_, f32[16,1024]{1,0:T(8,128)S(1)} %get-tuple-element.7.refs_1_), custom_call_target="tpu_custom_call" | custom-call | tf_op jit(solution)/shard_map/hand_over/pallas_call | solution.py:458

commit v2 on v1

--- a/solution.py
+++ b/solution.py
@@ -33,7 +33,7 @@
     hid_hbm, truth_hbm, lat_hbm, gain_hbm, w_hbm, wo_hbm,
     gh, gw_ref,
     hid, truth, lat, gain, wo_raw, w_full, normed, planes, inv_root, wo_pad, wo_t, hidden_act,
-    truth_pad, truth_t, area_t, act, fields, coarse, theirs, answers, pairs, gp,
+    truth_pad, truth_t, area_t, act, fields, coarse, theirs, answers, pairs, gp, parts,
     csend, crecv, sums, send1, recv1, send2, recv2, send3, recv3, finals,
     local_sem, a1_s, a1_r, a2_s, a2_r, a3_s, a3_r, a4_s, a4_r,
     b1_s, b1_r, b2_s, b2_r, c0_s, c0_r, c1_s, c1_r, c2_s, c2_r, c3_s, c3_r, c4_s, c4_r,
@@ -101,6 +101,15 @@
 
         lax.fori_loop(first, last, step, 0)
 
+    def by_rows(first, last, body):
+        chunks = math.gcd(4, (last - first) // 16)
+
+        def step(i):
+            for u in range(chunks):
+                body(rows_at(first + (i * chunks + u) * 16, 16))
+
+        loop(0, (last - first) // (16 * chunks), step)
+
     barrier = pltpu.get_barrier_semaphore()
 
     def greet(peer):
@@ -129,16 +138,14 @@
     loads[0].wait()
     loads[1].wait()
 
-    def normalise(i):
-        rows = rows_at(i * 32, 32)
+    def normalise(rows):
         values = hid[rows, :].astype(f32)
         root = jnp.sqrt(jnp.mean(values * values, axis=-1, keepdims=True) + EPSILON)
         inverse = 1.0 / root
-        inv_root[rows, :] = jnp.broadcast_to(inverse, (32, LANES))
+        inv_root[rows, :] = jnp.broadcast_to(inverse, (16, LANES))
         normed[rows, :] = (values * inverse * gain[...]).astype(bf16)
 
-    steps = points // 32
-    loop(0, steps, normalise)
+    by_rows(0, points, normalise)
     own_w.wait()
     z_blocks = w_full.at[0, 0, pl.ds(0, nh - 1), :, mine]
     drain(z_blocks, a1_r.at[0])
@@ -179,6 +186,14 @@
 
     loop(1, n, pass_first)
 
+    truth_t[...] = truth_pad[...].T
+    latitude = math.pi * ((lat[...].astype(f32) + 0.5) / LATS - 0.5)
+    area = LOSS_SCALE * jnp.cos(latitude)
+    strip = lat.shape[1]
+    for i in range(lat.shape[0]):
+        area_t[i * strip:(i + 1) * strip, :] = jnp.broadcast_to(area[i:i + 1, :], (LANES, strip)).T
+    wo_t[...] = wo_pad[...].T
+
     def pass_second(j):
         b = ordered(j)
         for i in range(2):
@@ -204,32 +219,25 @@
             preferred_element_type=f32,
         )
 
-    def activate(i, cols):
-        rows = rows_at(i * 32, 32)
+    def activate(rows, cols):
         a = act[rows, cols]
         hidden_act[rows, cols] = (a * (0.5 * jnp.tanh(0.5 * a) + 0.5)).astype(bf16)
 
     loop(0, tiles, lambda t: project(rows_at(t * tile, tile), mine))
-    loop(0, steps, lambda i: activate(i, mine))
-
-    truth_t[...] = truth_pad[...].T
-    latitude = math.pi * ((lat[...].astype(f32) + 0.5) / LATS - 0.5)
-    area = LOSS_SCALE * jnp.cos(latitude)
-    strip = lat.shape[1]
-    for i in range(lat.shape[0]):
-        area_t[i * strip:(i + 1) * strip, :] = jnp.broadcast_to(area[i:i + 1, :], (LANES, strip)).T
-    wo_t[...] = wo_pad[...].T
+    by_rows(0, points, lambda rows: activate(rows, mine))
+
     drain(w_full.at[:, :, :, :, other], a4_r.at[0])
 
     def share_of(t, m):
         return rows_at(t * tile + m * share, share)
 
-    tile_steps = tile // 32
+    def tile_rows(t, body):
+        by_rows(0, tile, lambda rows: body(rows_at(t * tile + rows.start, 16)))
 
     def forward(t):
         rows = rows_at(t * tile, tile)
         project(rows, other)
-        loop(t * tile_steps, (t + 1) * tile_steps, lambda i: activate(i, other))
+        tile_rows(t, lambda rows: activate(rows, other))
         field = jnp.dot(hidden_act[rows, :], wo_t[...], preferred_element_type=f32)
         fields[rows, :] = field
         coarse[rows, :] = field.astype(bf16)
@@ -246,8 +254,7 @@
 
     loop(0, tiles, forward)
 
-    def differentiate(i):
-        rows = rows_at(i * 32, 32)
+    def differentiate(rows):
         a = act[rows, :]
         s = 0.5 * jnp.tanh(0.5 * a) + 0.5
         act[rows, :] = s * (1.0 + a * (1.0 - s))
@@ -294,10 +301,10 @@
 
         loop(1, count, reply)
         pairs[share_of(t, member), :] = answers[t, member]
-        loop(t * tile_steps, (t + 1) * tile_steps, differentiate)
-        loop(t * turns // tiles, (t + 1) * turns // tiles, turn)
+        tile_rows(t, differentiate)
 
     loop(0, tiles, answer)
+    loop(0, turns, turn)
 
     fair = (1.0 - (1.0 - ALPHA) / count) / (count * (count - 1))
 
@@ -312,16 +319,30 @@
         grad_act = jnp.dot(grad_fields.astype(bf16), wo_pad[...], preferred_element_type=f32)
         gp[rows, :] = (grad_act * act[rows, :]).astype(bf16)
 
-    loop(0, tiles, backward)
-
     depth = width // n
+    early = (tiles - 1) * tile
 
     def nth(i, own):
         first = jnp.where(i == 0, (own + 2) % n, own + 1 - 2 * (own % 2))
         return jnp.where(i < 2, first, jnp.where(i == 2, n - 1 - own, own))
 
+    def product(which, i, begin, end):
+        plane, cols = (nth(i, p), mine) if which else (nth(i, q), other)
+        return jnp.dot(
+            planes[core if which else 1 - core, plane, :, begin:end], gp[begin:end, cols],
+            preferred_element_type=f32,
+        )
+
+    def early_planes(i):
+        for which in range(2):
+            parts[which, i] = product(which, i, 0, early)
+
+    loop(0, tiles - 1, backward)
+    loop(0, n, early_planes)
+    backward(tiles - 1)
+
     def other_plane(i):
-        part = jnp.dot(planes[1 - core, nth(i, q)], gp[:, other], preferred_element_type=f32)
+        part = parts[0, i] + product(0, i, early, points)
         csend[i] = part.astype(bf16)
         send(csend.at[i], crecv.at[i], c0_s.at[0], c0_r.at[i], partner)
 
@@ -333,7 +354,7 @@
         send(send1.at[slot], recv1.at[slot], c1_s.at[0], c1_r.at[slot], p_peers[target])
 
     def own_plane(i):
-        part = jnp.dot(planes[core, nth(i, p)], gp[:, mine], preferred_element_type=f32)
+        part = parts[1, i] + product(1, i, early, points)
         drain(crecv.at[i], c0_r.at[i])
         total = part + crecv[i].astype(f32)
         sums[i] = total
@@ -364,8 +385,7 @@
             preferred_element_type=f32,
         )
 
-    def hidden_grad(i):
-        rows = rows_at(i * 32, 32)
+    def hidden_grad(rows):
         scaled = act[rows, :] * gain[...]
         inverse = inv_root[rows, 0:1]
         unit = hid[rows, :].astype(f32) * inverse
@@ -407,7 +427,7 @@
         send3.at[(h + i // chips) % nh, (low + i % chips) % chips], recv3.at[i - 1],
         c3_s.at[0], c3_r.at[0], z_peer(i),
     ))
-    loop(0, steps // 2, hidden_grad)
+    by_rows(0, points // 2, hidden_grad)
     drain(recv3, c3_r.at[0])
     total = send3[h, low].astype(f32)
     for i in range(nh * chips - 1):
@@ -416,7 +436,7 @@
     finals[core * chips + low] = total * factor
     own_final = finals.at[core * chips + low]
     loop(1, count, lambda k: send(own_final, own_final, c4_s.at[0], c4_r.at[0], m_peer(k)))
-    loop(steps // 2, steps, hidden_grad)
+    by_rows(points // 2, points, hidden_grad)
     others = finals.at[pl.ds(0, count - 1)]
     drain(others, c4_r.at[0])
     for i in range(count):
@@ -501,6 +521,7 @@
         vmem((tiles, count, share, LANES), bf16),
         vmem((points, LANES), bf16),
         vmem((points, width), bf16),
+        vmem((2, n, width // n, half), f32),
         vmem((n, width // n, half), bf16),
         vmem((n, width // n, half), bf16),
         vmem((n, width // n, half), f32),

time: 80.7 us -> 81.4 us (level)
  no operation moved by 1% of the time
where the time goes in v2:
time: 81.4 us; the launch traced here: 81.3 us
  Pallas kernels  80.7 us (99%)
    pallas_call x1, Pallas kernels, per_device(): pl.pallas_call(functools.partial(kernel, tile), out_shape=(vmem((points,...  79.4 us

profile of v2, /device:TPU:1, one launch (start us, length us, event | category | flops | bytes accessed | tf_op | source)
XLA Modules:
  0.0 81.3 jit_solution(14922209199522721095)
XLA Ops:
  0.6 79.4 %crps_step.1 = (bf16[768,1024]{1,0:T(8,128)(2,1)S(1)}, f32[16,1024]{1,0:T(8,128)S(1)}) custom-call(bf16[768,1024]{1,0:T(8,128)(2,1)} %bitcast.4, f32[100,768]{1,0:T(8,128)} %truth_hbm.1, s32[6,128]{1,0:T(8,128)} %bitcast.5, f32[1,1024]{1,0:T(1,128)} %bitcast.6, bf16[16,1024]{1,0:T(8,128)(2,1)} %w_hbm.1, bf16[100,1024]{1,0:T(8,128)(2,1)} %wo_hbm.1), custom_call_target="tpu_custom_call" | custom-call | tf_op jit(solution)/shard_map/crps_step/pallas_call | solution.py:543
  80.1 1.2 %hand_over.1 = (bf16[768,1024]{1,0:T(8,128)(2,1)}, f32[16,1024]{1,0:T(8,128)}) custom-call(bf16[768,1024]{1,0:T(8,128)(2,1)S(1)} %get-tuple-element.6.refs_0_, f32[16,1024]{1,0:T(8,128)S(1)} %get-tuple-element.7.refs_1_), custom_call_target="tpu_custom_call" | custom-call | tf_op jit(solution)/shard_map/hand_over/pallas_call | solution.py:478

commit v3 on v2

--- a/solution.py
+++ b/solution.py
@@ -150,115 +150,6 @@
     z_blocks = w_full.at[0, 0, pl.ds(0, nh - 1), :, mine]
     drain(z_blocks, a1_r.at[0])
 
-    def group(p_, b, cols=mine):
-        x_, y_ = place(p_, (q - b + n) % n)
-        return w_full.at[x_, :, y_, :, cols]
-
-    def to_partner(p_, b):
-        part = group(p_, b)
-        send(part, part, a4_s.at[0], a4_r.at[0], partner)
-
-    def to_second(b):
-        part = group(p, b)
-        for i in range(2):
-            send(part, part, a3_s.at[0], a3_r.at[b, i], p_peers[i])
-        to_partner(p, b)
-
-    def ordered(j):
-        return j + (j // 2) * (n + 1 - 2 * j)
-
-    own_group = group(p, 0)
-    loop(1, n, lambda j: send(
-        own_group, own_group, a2_s.at[0], a2_r.at[ordered(j) - 1], q_peer(ordered(j))
-    ))
-    to_second(0)
-    for load in loads[2:]:
-        load.wait()
-    truth_pad[...] = jnp.zeros_like(truth_pad)
-    truth_pad[0:levels, :] = truth[...]
-    wo_pad[...] = jnp.zeros_like(wo_pad)
-    wo_pad[0:levels, :] = wo_raw[...]
-
-    def pass_first(j):
-        b = ordered(j)
-        drain(own_group, a2_r.at[b - 1])
-        to_second(b)
-
-    loop(1, n, pass_first)
-
-    truth_t[...] = truth_pad[...].T
-    latitude = math.pi * ((lat[...].astype(f32) + 0.5) / LATS - 0.5)
-    area = LOSS_SCALE * jnp.cos(latitude)
-    strip = lat.shape[1]
-    for i in range(lat.shape[0]):
-        area_t[i * strip:(i + 1) * strip, :] = jnp.broadcast_to(area[i:i + 1, :], (LANES, strip)).T
-    wo_t[...] = wo_pad[...].T
-
-    def pass_second(j):
-        b = ordered(j)
-        for i in range(2):
-            drain(own_group, a3_r.at[b, i])
-            part = group(sides[i], b, quarters[i])
-            send(part, part, a3_s.at[0], a3_r.at[b, 2 + i], p_peers[1 - i])
-        for i in range(2):
-            to_partner(sides[i], b)
-
-    loop(0, n, pass_second)
-
-    def pass_far(j):
-        b = ordered(j)
-        for i in range(2):
-            drain(group(far, b, quarters[i]), a3_r.at[b, 2 + i])
-        to_partner(far, b)
-
-    loop(0, n, pass_far)
-
-    def project(rows, cols):
-        act[rows, cols] = jnp.dot(
-            normed[rows, :], w_full[:, :, :, :, cols].reshape(width, half),
-            preferred_element_type=f32,
-        )
-
-    def activate(rows, cols):
-        a = act[rows, cols]
-        hidden_act[rows, cols] = (a * (0.5 * jnp.tanh(0.5 * a) + 0.5)).astype(bf16)
-
-    loop(0, tiles, lambda t: project(rows_at(t * tile, tile), mine))
-    by_rows(0, points, lambda rows: activate(rows, mine))
-
-    drain(w_full.at[:, :, :, :, other], a4_r.at[0])
-
-    def share_of(t, m):
-        return rows_at(t * tile + m * share, share)
-
-    def tile_rows(t, body):
-        by_rows(0, tile, lambda rows: body(rows_at(t * tile + rows.start, 16)))
-
-    def forward(t):
-        rows = rows_at(t * tile, tile)
-        project(rows, other)
-        tile_rows(t, lambda rows: activate(rows, other))
-        field = jnp.dot(hidden_act[rows, :], wo_t[...], preferred_element_type=f32)
-        fields[rows, :] = field
-        coarse[rows, :] = field.astype(bf16)
-
-        def spread(k):
-            peer = m_peer(k)
-            send(
-                coarse.at[share_of(t, peer[0]), :], theirs.at[t, member],
-                b1_s.at[0], b1_r.at[t], peer,
-            )
-
-        loop(1, count, spread)
-        theirs[t, member] = coarse[share_of(t, member), :]
-
-    loop(0, tiles, forward)
-
-    def differentiate(rows):
-        a = act[rows, :]
-        s = 0.5 * jnp.tanh(0.5 * a) + 0.5
-        act[rows, :] = s * (1.0 + a * (1.0 - s))
-
     span = min(LANES, points)
     turns = points // span
 
@@ -274,6 +165,111 @@
                     planes[0, y_, to_x:to_x + block, cols] = piece
                     planes[1, x_, to_y:to_y + block, cols] = piece
 
+    def group(p_, b, cols=mine):
+        x_, y_ = place(p_, (q - b + n) % n)
+        return w_full.at[x_, :, y_, :, cols]
+
+    def to_partner(p_, b):
+        part = group(p_, b)
+        send(part, part, a4_s.at[0], a4_r.at[0], partner)
+
+    def to_second(b):
+        part = group(p, b)
+        for i in range(2):
+            send(part, part, a3_s.at[0], a3_r.at[b, i], p_peers[i])
+        to_partner(p, b)
+
+    def ordered(j):
+        return j + (j // 2) * (n + 1 - 2 * j)
+
+    own_group = group(p, 0)
+    loop(1, n, lambda j: send(
+        own_group, own_group, a2_s.at[0], a2_r.at[ordered(j) - 1], q_peer(ordered(j))
+    ))
+    to_second(0)
+    loop(0, turns // 3, turn)
+    for load in loads[2:]:
+        load.wait()
+    truth_pad[...] = jnp.zeros_like(truth_pad)
+    truth_pad[0:levels, :] = truth[...]
+    wo_pad[...] = jnp.zeros_like(wo_pad)
+    wo_pad[0:levels, :] = wo_raw[...]
+
+    def pass_first(j):
+        b = ordered(j)
+        drain(own_group, a2_r.at[b - 1])
+        to_second(b)
+
+    loop(1, n, pass_first)
+    loop(turns // 3, 2 * turns // 3, turn)
+
+    truth_t[...] = truth_pad[...].T
+    latitude = math.pi * ((lat[...].astype(f32) + 0.5) / LATS - 0.5)
+    area = LOSS_SCALE * jnp.cos(latitude)
+    strip = lat.shape[1]
+    for i in range(lat.shape[0]):
+        area_t[i * strip:(i + 1) * strip, :] = jnp.broadcast_to(area[i:i + 1, :], (LANES, strip)).T
+    wo_t[...] = wo_pad[...].T
+
+    def pass_second(j):
+        b = ordered(j)
+        for i in range(2):
+            drain(own_group, a3_r.at[b, i])
+            part = group(sides[i], b, quarters[i])
+            send(part, part, a3_s.at[0], a3_r.at[b, 2 + i], p_peers[1 - i])
+        for i in range(2):
+            to_partner(sides[i], b)
+
+    loop(0, n, pass_second)
+    loop(2 * turns // 3, turns, turn)
+
+    def pass_far(j):
+        b = ordered(j)
+        for i in range(2):
+            drain(group(far, b, quarters[i]), a3_r.at[b, 2 + i])
+        to_partner(far, b)
+
+    loop(0, n, pass_far)
+
+    def project(rows, cols):
+        act[rows, cols] = jnp.dot(
+            normed[rows, :], w_full[:, :, :, :, cols].reshape(width, half),
+            preferred_element_type=f32,
+        )
+
+    def activate(rows, cols):
+        a = act[rows, cols]
+        hidden_act[rows, cols] = (a * (0.5 * jnp.tanh(0.5 * a) + 0.5)).astype(bf16)
+
+    loop(0, tiles, lambda t: project(rows_at(t * tile, tile), mine))
+    by_rows(0, points, lambda rows: activate(rows, mine))
+
+    drain(w_full.at[:, :, :, :, other], a4_r.at[0])
+
+    def share_of(t, m):
+        return rows_at(t * tile + m * share, share)
+
+    def tile_rows(t, body):
+        by_rows(0, tile, lambda rows: body(rows_at(t * tile + rows.start, 16)))
+
+    def forward(t):
+        rows = rows_at(t * tile, tile)
+        project(rows, other)
+        tile_rows(t, lambda rows: activate(rows, other))
+        field = jnp.dot(hidden_act[rows, :], wo_t[...], preferred_element_type=f32)
+        fields[rows, :] = field
+        coarse[rows, :] = field.astype(bf16)
+
+        def spread(k):
+            peer = m_peer(k)
+            send(
+                coarse.at[share_of(t, peer[0]), :], theirs.at[t, member],
+                b1_s.at[0], b1_r.at[t], peer,
+            )
+
+        loop(1, count, spread)
+        theirs[t, member] = coarse[share_of(t, member), :]
+
     def answer(t):
         come = theirs.at[t, pl.ds(0, count - 1)]
         drain(come, b1_r.at[t])
@@ -301,10 +297,22 @@
 
         loop(1, count, reply)
         pairs[share_of(t, member), :] = answers[t, member]
-        tile_rows(t, differentiate)
-
-    loop(0, tiles, answer)
-    loop(0, turns, turn)
+
+
+    def differentiate(rows):
+        a = act[rows, :]
+        s = 0.5 * jnp.tanh(0.5 * a) + 0.5
+        act[rows, :] = s * (1.0 + a * (1.0 - s))
+
+    loop(0, tiles - 1, forward)
+    if tiles > 1:
+        loop(0, tiles - 2, answer)
+    forward(tiles - 1)
+    if tiles > 1:
+        answer(tiles - 2)
+    tile_rows(0, differentiate)
+    answer(tiles - 1)
+    by_rows(tile, points, differentiate)
 
     fair = (1.0 - (1.0 - ALPHA) / count) / (count * (count - 1))
 

time: 81.4 us -> 82.5 us (1.014)
  Pallas kernels: 80.7 us -> 81.7 us
    pallas_call x1, Pallas kernels: 79.4 us -> 80.5 us  [per_device(): pl.pallas_call(functools.partial(kernel, tile), out_shape=(vmem((points,...]
where the time goes in v3:
time: 82.5 us; the launch traced here: 82.4 us
  Pallas kernels  81.7 us (99%)
    pallas_call x1, Pallas kernels, per_device(): pl.pallas_call(functools.partial(kernel, tile), out_shape=(vmem((points,...  80.5 us

profile of v3, /device:TPU:1, one launch (start us, length us, event | category | flops | bytes accessed | tf_op | source)
XLA Modules:
  0.0 82.4 jit_solution(1214307775124810001)
XLA Ops:
  0.6 80.5 %crps_step.1 = (bf16[768,1024]{1,0:T(8,128)(2,1)S(1)}, f32[16,1024]{1,0:T(8,128)S(1)}) custom-call(bf16[768,1024]{1,0:T(8,128)(2,1)} %bitcast.4, f32[100,768]{1,0:T(8,128)} %truth_hbm.1, s32[6,128]{1,0:T(8,128)} %bitcast.5, f32[1,1024]{1,0:T(1,128)} %bitcast.6, bf16[16,1024]{1,0:T(8,128)(2,1)} %w_hbm.1, bf16[100,1024]{1,0:T(8,128)(2,1)} %wo_hbm.1), custom_call_target="tpu_custom_call" | custom-call | tf_op jit(solution)/shard_map/crps_step/pallas_call | solution.py:551
  81.2 1.2 %hand_over.1 = (bf16[768,1024]{1,0:T(8,128)(2,1)}, f32[16,1024]{1,0:T(8,128)}) custom-call(bf16[768,1024]{1,0:T(8,128)(2,1)S(1)} %get-tuple-element.6.refs_0_, f32[16,1024]{1,0:T(8,128)S(1)} %get-tuple-element.7.refs_1_), custom_call_target="tpu_custom_call" | custom-call | tf_op jit(solution)/shard_map/hand_over/pallas_call | solution.py:486

commit v4 on v3

--- a/solution.py
+++ b/solution.py
@@ -33,7 +33,7 @@
     hid_hbm, truth_hbm, lat_hbm, gain_hbm, w_hbm, wo_hbm,
     gh, gw_ref,
     hid, truth, lat, gain, wo_raw, w_full, normed, planes, inv_root, wo_pad, wo_t, hidden_act,
-    truth_pad, truth_t, area_t, act, fields, coarse, theirs, answers, pairs, gp, parts,
+    truth_pad, truth_t, area_t, act, fields, coarse, theirs, answers, pairs, gp,
     csend, crecv, sums, send1, recv1, send2, recv2, send3, recv3, finals,
     local_sem, a1_s, a1_r, a2_s, a2_r, a3_s, a3_r, a4_s, a4_r,
     b1_s, b1_r, b2_s, b2_r, c0_s, c0_r, c1_s, c1_r, c2_s, c2_r, c3_s, c3_r, c4_s, c4_r,
@@ -134,7 +134,26 @@
     pl.semaphore_wait(barrier, nh * chips - chips + n - 1 + 2 + count - 1)
 
     own_block = w_full.at[x, h, y, :, mine]
-    loop(1, nh, lambda k: send(w_hbm.at[:, mine], own_block, a1_s.at[0], a1_r.at[0], h_peer(k)))
+    def to_z(dh, l_):
+        target = (2 * l_ + core, (x * nh + (h + dh) % nh) * ny + y)
+        send(w_hbm.at[:, mine], own_block, a1_s.at[0], a1_r.at[0], target)
+
+    ends = ((chips - 1, 1, 0), (0, nh - 1, chips // 2))
+
+    def from_end(action):
+        for end, toward, start in ends:
+            @pl.when(low == end)
+            def _():
+                action(toward, start)
+
+    def spread_z(toward, start):
+        loop(0, chips, lambda l_: to_z(toward, l_))
+        loop(start, start + chips // 2, lambda l_: to_z(2, l_))
+
+    if chips == 1:
+        loop(1, nh, lambda k: to_z(k, 0))
+    else:
+        from_end(spread_z)
     loads[0].wait()
     loads[1].wait()
 
@@ -146,9 +165,11 @@
         normed[rows, :] = (values * inverse * gain[...]).astype(bf16)
 
     by_rows(0, points, normalise)
-    own_w.wait()
-    z_blocks = w_full.at[0, 0, pl.ds(0, nh - 1), :, mine]
-    drain(z_blocks, a1_r.at[0])
+    for load in loads[2:]:
+        load.wait()
+    wo_pad[...] = jnp.zeros_like(wo_pad)
+    wo_pad[0:levels, :] = wo_raw[...]
+    wo_t[...] = wo_pad[...].T
 
     span = min(LANES, points)
     turns = points // span
@@ -165,6 +186,11 @@
                     planes[0, y_, to_x:to_x + block, cols] = piece
                     planes[1, x_, to_y:to_y + block, cols] = piece
 
+    loop(0, turns // 2, turn)
+    own_w.wait()
+    z_blocks = w_full.at[0, 0, pl.ds(0, nh - 1), :, mine]
+    drain(z_blocks, a1_r.at[0])
+
     def group(p_, b, cols=mine):
         x_, y_ = place(p_, (q - b + n) % n)
         return w_full.at[x_, :, y_, :, cols]
@@ -187,29 +213,12 @@
         own_group, own_group, a2_s.at[0], a2_r.at[ordered(j) - 1], q_peer(ordered(j))
     ))
     to_second(0)
-    loop(0, turns // 3, turn)
-    for load in loads[2:]:
-        load.wait()
-    truth_pad[...] = jnp.zeros_like(truth_pad)
-    truth_pad[0:levels, :] = truth[...]
-    wo_pad[...] = jnp.zeros_like(wo_pad)
-    wo_pad[0:levels, :] = wo_raw[...]
-
     def pass_first(j):
         b = ordered(j)
         drain(own_group, a2_r.at[b - 1])
         to_second(b)
 
     loop(1, n, pass_first)
-    loop(turns // 3, 2 * turns // 3, turn)
-
-    truth_t[...] = truth_pad[...].T
-    latitude = math.pi * ((lat[...].astype(f32) + 0.5) / LATS - 0.5)
-    area = LOSS_SCALE * jnp.cos(latitude)
-    strip = lat.shape[1]
-    for i in range(lat.shape[0]):
-        area_t[i * strip:(i + 1) * strip, :] = jnp.broadcast_to(area[i:i + 1, :], (LANES, strip)).T
-    wo_t[...] = wo_pad[...].T
 
     def pass_second(j):
         b = ordered(j)
@@ -221,7 +230,6 @@
             to_partner(sides[i], b)
 
     loop(0, n, pass_second)
-    loop(2 * turns // 3, turns, turn)
 
     def pass_far(j):
         b = ordered(j)
@@ -241,8 +249,9 @@
         a = act[rows, cols]
         hidden_act[rows, cols] = (a * (0.5 * jnp.tanh(0.5 * a) + 0.5)).astype(bf16)
 
-    loop(0, tiles, lambda t: project(rows_at(t * tile, tile), mine))
-    by_rows(0, points, lambda rows: activate(rows, mine))
+    ahead = max(tiles - 1, 1)
+    loop(0, ahead, lambda t: project(rows_at(t * tile, tile), mine))
+    by_rows(0, ahead * tile, lambda rows: activate(rows, mine))
 
     drain(w_full.at[:, :, :, :, other], a4_r.at[0])
 
@@ -304,15 +313,27 @@
         s = 0.5 * jnp.tanh(0.5 * a) + 0.5
         act[rows, :] = s * (1.0 + a * (1.0 - s))
 
-    loop(0, tiles - 1, forward)
-    if tiles > 1:
-        loop(0, tiles - 2, answer)
-    forward(tiles - 1)
-    if tiles > 1:
-        answer(tiles - 2)
-    tile_rows(0, differentiate)
-    answer(tiles - 1)
-    by_rows(tile, points, differentiate)
+    loop(0, ahead, forward)
+    truth_pad[...] = jnp.zeros_like(truth_pad)
+    truth_pad[0:levels, :] = truth[...]
+    truth_t[...] = truth_pad[...].T
+    latitude = math.pi * ((lat[...].astype(f32) + 0.5) / LATS - 0.5)
+    area = LOSS_SCALE * jnp.cos(latitude)
+    strip = lat.shape[1]
+    for i in range(lat.shape[0]):
+        area_t[i * strip:(i + 1) * strip, :] = jnp.broadcast_to(area[i:i + 1, :], (LANES, strip)).T
+    if ahead < tiles:
+        project(rows_at(ahead * tile, tile), mine)
+        tile_rows(ahead, lambda rows: activate(rows, mine))
+        forward(ahead)
+
+    def reply_and_prepare(t):
+        answer(t)
+        tile_rows(t, differentiate)
+        left = turns - turns // 2
+        loop(turns // 2 + t * left // tiles, turns // 2 + (t + 1) * left // tiles, turn)
+
+    loop(0, tiles, reply_and_prepare)
 
     fair = (1.0 - (1.0 - ALPHA) / count) / (count * (count - 1))
 
@@ -328,29 +349,21 @@
         gp[rows, :] = (grad_act * act[rows, :]).astype(bf16)
 
     depth = width // n
-    early = (tiles - 1) * tile
 
     def nth(i, own):
         first = jnp.where(i == 0, (own + 2) % n, own + 1 - 2 * (own % 2))
         return jnp.where(i < 2, first, jnp.where(i == 2, n - 1 - own, own))
 
-    def product(which, i, begin, end):
+    def product(which, i):
         plane, cols = (nth(i, p), mine) if which else (nth(i, q), other)
         return jnp.dot(
-            planes[core if which else 1 - core, plane, :, begin:end], gp[begin:end, cols],
-            preferred_element_type=f32,
+            planes[core if which else 1 - core, plane], gp[:, cols], preferred_element_type=f32
         )
 
-    def early_planes(i):
-        for which in range(2):
-            parts[which, i] = product(which, i, 0, early)
-
-    loop(0, tiles - 1, backward)
-    loop(0, n, early_planes)
-    backward(tiles - 1)
+    loop(0, tiles, backward)
 
     def other_plane(i):
-        part = parts[0, i] + product(0, i, early, points)
+        part = product(0, i)
         csend[i] = part.astype(bf16)
         send(csend.at[i], crecv.at[i], c0_s.at[0], c0_r.at[i], partner)
 
@@ -362,7 +375,7 @@
         send(send1.at[slot], recv1.at[slot], c1_s.at[0], c1_r.at[slot], p_peers[target])
 
     def own_plane(i):
-        part = parts[1, i] + product(1, i, early, points)
+        part = product(1, i)
         drain(crecv.at[i], c0_r.at[i])
         total = part + crecv[i].astype(f32)
         sums[i] = total
@@ -450,7 +463,10 @@
     for i in range(count):
         gw_ref[:, i * strip:(i + 1) * strip] = finals[i]
 
-    drain(z_blocks, a1_s.at[0])
+    if chips == 1:
+        drain(z_blocks, a1_s.at[0])
+    else:
+        from_end(lambda toward, start: [drain(z_blocks, a1_s.at[0]) for _ in range(2)])
     drain(w_full.at[pl.ds(0, n - 1), :, 0, :, mine], a2_s.at[0])
     drain(w_full.at[:, :, pl.ds(0, 3), :, mine], a3_s.at[0])
     drain(w_full.at[:, :, :, :, mine], a4_s.at[0])
@@ -529,7 +545,6 @@
         vmem((tiles, count, share, LANES), bf16),
         vmem((points, LANES), bf16),
         vmem((points, width), bf16),
-        vmem((2, n, width // n, half), f32),
         vmem((n, width // n, half), bf16),
         vmem((n, width // n, half), bf16),
         vmem((n, width // n, half), f32),

time: 82.5 us -> 78 us (0.945)
  Pallas kernels: 81.7 us -> 77.2 us
    pallas_call x1, Pallas kernels: 80.5 us -> 76 us  [per_device(): pl.pallas_call(functools.partial(kernel, tile), out_shape=(vmem((points,...]
where the time goes in v4:
time: 78 us; the launch traced here: 77.9 us
  Pallas kernels  77.2 us (99%)
    pallas_call x1, Pallas kernels, per_device(): pl.pallas_call(functools.partial(kernel, tile), out_shape=(vmem((points,...  76 us

profile of v4, /device:TPU:1, one launch (start us, length us, event | category | flops | bytes accessed | tf_op | source)
XLA Modules:
  0.0 77.9 jit_solution(14672268378894385140)
XLA Ops:
  0.6 76.0 %crps_step.1 = (bf16[768,1024]{1,0:T(8,128)(2,1)S(1)}, f32[16,1024]{1,0:T(8,128)S(1)}) custom-call(bf16[768,1024]{1,0:T(8,128)(2,1)} %bitcast.4, f32[100,768]{1,0:T(8,128)} %truth_hbm.1, s32[6,128]{1,0:T(8,128)} %bitcast.5, f32[1,1024]{1,0:T(1,128)} %bitcast.6, bf16[16,1024]{1,0:T(8,128)(2,1)} %w_hbm.1, bf16[100,1024]{1,0:T(8,128)(2,1)} %wo_hbm.1), custom_call_target="tpu_custom_call" | custom-call | tf_op jit(solution)/shard_map/crps_step/pallas_call | solution.py:566
  76.7 1.2 %hand_over.1 = (bf16[768,1024]{1,0:T(8,128)(2,1)}, f32[16,1024]{1,0:T(8,128)}) custom-call(bf16[768,1024]{1,0:T(8,128)(2,1)S(1)} %get-tuple-element.6.refs_0_, f32[16,1024]{1,0:T(8,128)S(1)} %get-tuple-element.7.refs_1_), custom_call_target="tpu_custom_call" | custom-call | tf_op jit(solution)/shard_map/hand_over/pallas_call | solution.py:502

commit v5 on v4

--- a/solution.py
+++ b/solution.py
@@ -16,7 +16,7 @@
 
 GRID = (4, 4, 4)
 LANES = 128
-TILE = 256
+TILES = (128, 256, 256, 128)
 MESH = pl.DeviceIdType.MESH
 
 
@@ -29,7 +29,7 @@
 
 
 def kernel(
-    tile,
+    sizes,
     hid_hbm, truth_hbm, lat_hbm, gain_hbm, w_hbm, wo_hbm,
     gh, gw_ref,
     hid, truth, lat, gain, wo_raw, w_full, normed, planes, inv_root, wo_pad, wo_t, hidden_act,
@@ -47,7 +47,9 @@
     count = finals.shape[0]
     chips = count // 2
     block = w_full.shape[3]
-    tiles, share = theirs.shape[0], theirs.shape[2]
+    tiles = len(sizes)
+    starts = [sum(sizes[:t]) for t in range(tiles)]
+    shares = [size // count for size in sizes]
     f32, bf16 = jnp.float32, jnp.bfloat16
 
     member, space = lax.axis_index("member"), lax.axis_index("space")
@@ -128,8 +130,7 @@
             [(hid_hbm, hid), (gain_hbm, gain), (truth_hbm, truth), (lat_hbm, lat), (wo_hbm, wo_raw)]
         )
     ]
-    own_w.start()
-    for load in loads:
+    for load in loads[:2]:
         load.start()
     pl.semaphore_wait(barrier, nh * chips - chips + n - 1 + 2 + count - 1)
 
@@ -154,6 +155,9 @@
         loop(1, nh, lambda k: to_z(k, 0))
     else:
         from_end(spread_z)
+    own_w.start()
+    for load in loads[2:]:
+        load.start()
     loads[0].wait()
     loads[1].wait()
 
@@ -218,7 +222,6 @@
         drain(own_group, a2_r.at[b - 1])
         to_second(b)
 
-    loop(1, n, pass_first)
 
     def pass_second(j):
         b = ordered(j)
@@ -229,7 +232,9 @@
         for i in range(2):
             to_partner(sides[i], b)
 
-    loop(0, n, pass_second)
+    pass_second(0)
+    loop(1, n, pass_first)
+    loop(1, n, pass_second)
 
     def pass_far(j):
         b = ordered(j)
@@ -249,22 +254,25 @@
         a = act[rows, cols]
         hidden_act[rows, cols] = (a * (0.5 * jnp.tanh(0.5 * a) + 0.5)).astype(bf16)
 
+    def own_half(t):
+        project(pl.ds(starts[t], sizes[t]), mine)
+        by_rows(starts[t], starts[t] + sizes[t], lambda rows: activate(rows, mine))
+
     ahead = max(tiles - 1, 1)
-    loop(0, ahead, lambda t: project(rows_at(t * tile, tile), mine))
-    by_rows(0, ahead * tile, lambda rows: activate(rows, mine))
-
+    for t in range(ahead):
+        own_half(t)
     drain(w_full.at[:, :, :, :, other], a4_r.at[0])
 
     def share_of(t, m):
-        return rows_at(t * tile + m * share, share)
-
-    def tile_rows(t, body):
-        by_rows(0, tile, lambda rows: body(rows_at(t * tile + rows.start, 16)))
+        return rows_at(starts[t] + m * shares[t], shares[t])
+
+    def slot(t):
+        return pl.ds(starts[t] // count, shares[t])
 
     def forward(t):
-        rows = rows_at(t * tile, tile)
+        rows = pl.ds(starts[t], sizes[t])
         project(rows, other)
-        tile_rows(t, lambda rows: activate(rows, other))
+        by_rows(starts[t], starts[t] + sizes[t], lambda part: activate(part, other))
         field = jnp.dot(hidden_act[rows, :], wo_t[...], preferred_element_type=f32)
         fields[rows, :] = field
         coarse[rows, :] = field.astype(bf16)
@@ -272,20 +280,20 @@
         def spread(k):
             peer = m_peer(k)
             send(
-                coarse.at[share_of(t, peer[0]), :], theirs.at[t, member],
+                coarse.at[share_of(t, peer[0]), :], theirs.at[member, slot(t), :],
                 b1_s.at[0], b1_r.at[t], peer,
             )
 
         loop(1, count, spread)
-        theirs[t, member] = coarse[share_of(t, member), :]
+        theirs[member, slot(t), :] = coarse[share_of(t, member), :]
 
     def answer(t):
-        come = theirs.at[t, pl.ds(0, count - 1)]
+        come = theirs.at[pl.ds(0, count - 1), slot(t), :]
         drain(come, b1_r.at[t])
 
         def compare(i):
-            rows = rows_at(i * 16, 16)
-            values = [theirs[t, m, rows, :].astype(f32) for m in range(count)]
+            rows = rows_at(starts[t] // count + i * 16, 16)
+            values = [theirs[m, rows, :].astype(f32) for m in range(count)]
             totals = [jnp.zeros_like(values[0]) for m in range(count)]
             for m in range(count):
                 for o in range(m + 1, count):
@@ -293,27 +301,28 @@
                     totals[m] = totals[m] + s
                     totals[o] = totals[o] - s
             for m in range(count):
-                answers[t, m, rows, :] = totals[m].astype(bf16)
-
-        loop(0, share // 16, compare)
+                answers[m, rows, :] = totals[m].astype(bf16)
+
+        loop(0, shares[t] // 16, compare)
 
         def reply(k):
             peer = m_peer(k)
             send(
-                answers.at[t, peer[0]], pairs.at[share_of(t, member), :],
+                answers.at[peer[0], slot(t), :], pairs.at[share_of(t, member), :],
                 b2_s.at[0], b2_r.at[t], peer,
             )
 
         loop(1, count, reply)
-        pairs[share_of(t, member), :] = answers[t, member]
-
+        pairs[share_of(t, member), :] = answers[member, slot(t), :]
 
     def differentiate(rows):
         a = act[rows, :]
         s = 0.5 * jnp.tanh(0.5 * a) + 0.5
         act[rows, :] = s * (1.0 + a * (1.0 - s))
 
-    loop(0, ahead, forward)
+    early = max(tiles - 2, 1)
+    for t in range(early):
+        forward(t)
     truth_pad[...] = jnp.zeros_like(truth_pad)
     truth_pad[0:levels, :] = truth[...]
     truth_t[...] = truth_pad[...].T
@@ -322,25 +331,31 @@
     strip = lat.shape[1]
     for i in range(lat.shape[0]):
         area_t[i * strip:(i + 1) * strip, :] = jnp.broadcast_to(area[i:i + 1, :], (LANES, strip)).T
-    if ahead < tiles:
-        project(rows_at(ahead * tile, tile), mine)
-        tile_rows(ahead, lambda rows: activate(rows, mine))
-        forward(ahead)
-
-    def reply_and_prepare(t):
+    for t in range(early, tiles):
+        if t == ahead:
+            own_half(t)
+        forward(t)
+        answer(t - early)
+
+    left = turns - turns // 2
+    done = 0
+
+    def prepare(t):
+        by_rows(starts[t], starts[t] + sizes[t], differentiate)
+
+    for t in range(tiles - early, tiles):
+        prepare(t - (tiles - early))
+        loop(turns // 2 + done * left // early, turns // 2 + (done + 1) * left // early, turn)
+        done += 1
         answer(t)
-        tile_rows(t, differentiate)
-        left = turns - turns // 2
-        loop(turns // 2 + t * left // tiles, turns // 2 + (t + 1) * left // tiles, turn)
-
-    loop(0, tiles, reply_and_prepare)
+    for t in range(early, tiles):
+        prepare(t)
 
     fair = (1.0 - (1.0 - ALPHA) / count) / (count * (count - 1))
 
     def backward(t):
-        come = pairs.at[pl.ds(0, tile - share), :]
-        drain(come, b2_r.at[t])
-        rows = rows_at(t * tile, tile)
+        drain(pairs.at[pl.ds(0, sizes[t] - shares[t]), :], b2_r.at[t])
+        rows = pl.ds(starts[t], sizes[t])
         grad_fields = area_t[rows, :] * (
             slope(fields[rows, :] - truth_t[rows, :]) * (1.0 / count)
             - fair * pairs[rows, :].astype(f32)
@@ -360,7 +375,8 @@
             planes[core if which else 1 - core, plane], gp[:, cols], preferred_element_type=f32
         )
 
-    loop(0, tiles, backward)
+    for t in range(tiles):
+        backward(t)
 
     def other_plane(i):
         part = product(0, i)
@@ -454,14 +470,14 @@
     for i in range(nh * chips - 1):
         total = total + recv3[i].astype(f32)
     factor = 1.0 / math.sqrt(count * points * nx * nh * ny)
-    finals[core * chips + low] = total * factor
+    finals[core * chips + low] = (total * factor).astype(bf16)
     own_final = finals.at[core * chips + low]
     loop(1, count, lambda k: send(own_final, own_final, c4_s.at[0], c4_r.at[0], m_peer(k)))
     by_rows(points // 2, points, hidden_grad)
     others = finals.at[pl.ds(0, count - 1)]
     drain(others, c4_r.at[0])
     for i in range(count):
-        gw_ref[:, i * strip:(i + 1) * strip] = finals[i]
+        gw_ref[:, i * strip:(i + 1) * strip] = finals[i].astype(f32)
 
     if chips == 1:
         drain(z_blocks, a1_s.at[0])
@@ -517,8 +533,8 @@
     levels = truth.shape[0]
     block = w_in.shape[0]
     half = width // 2
-    tile = min(TILE, points)
-    tiles, share = points // tile, tile // count
+    sizes = TILES if sum(TILES) == points else (points,)
+    tiles = len(sizes)
     f32, bf16 = jnp.float32, jnp.bfloat16
     vmem, dma = pltpu.VMEM, pltpu.SemaphoreType.DMA
     n, chips, lat_strip = nx, count // 2, min(LANES, points)
@@ -541,8 +557,8 @@
         vmem((points, width), f32),
         vmem((points, LANES), f32),
         vmem((points, LANES), bf16),
-        vmem((tiles, count, share, LANES), bf16),
-        vmem((tiles, count, share, LANES), bf16),
+        vmem((count, points // count, LANES), bf16),
+        vmem((count, points // count, LANES), bf16),
         vmem((points, LANES), bf16),
         vmem((points, width), bf16),
         vmem((n, width // n, half), bf16),
@@ -554,7 +570,7 @@
         vmem((n - 1, nh * block, half), bf16),
         vmem((nh, chips, block, half // chips), bf16),
         vmem((nh * chips - 1, block, half // chips), bf16),
-        vmem((count, block, half // chips), f32),
+        vmem((count, block, half // chips), bf16),
         dma((6,)),
     ]
     for arrivals in (
@@ -564,7 +580,7 @@
     ):
         scratch += [dma((1,)), dma(arrivals)]
     grad_rows, grad_first = pl.pallas_call(
-        functools.partial(kernel, tile),
+        functools.partial(kernel, sizes),
         out_shape=(
             vmem((points, width), bf16),
             vmem((block, width), f32),

time: 78 us -> 81.1 us (1.040)
  Pallas kernels: 77.2 us -> 80.3 us
    pallas_call x1, Pallas kernels: 76 us -> 79.1 us  [per_device(): pl.pallas_call(functools.partial(kernel, sizes), out_shape=(vmem((points,...]
where the time goes in v5:
time: 81.1 us; the launch traced here: 81 us
  Pallas kernels  80.3 us (99%)
    pallas_call x1, Pallas kernels, per_device(): pl.pallas_call(functools.partial(kernel, sizes), out_shape=(vmem((points,...  79.1 us

profile of v5, /device:TPU:1, one launch (start us, length us, event | category | flops | bytes accessed | tf_op | source)
XLA Modules:
  0.0 81.0 jit_solution(15529643136828964617)
XLA Ops:
  0.6 79.1 %crps_step.1 = (bf16[768,1024]{1,0:T(8,128)(2,1)S(1)}, f32[16,1024]{1,0:T(8,128)S(1)}) custom-call(bf16[768,1024]{1,0:T(8,128)(2,1)} %bitcast.4, f32[100,768]{1,0:T(8,128)} %truth_hbm.1, s32[6,128]{1,0:T(8,128)} %bitcast.5, f32[1,1024]{1,0:T(1,128)} %bitcast.6, bf16[16,1024]{1,0:T(8,128)(2,1)} %w_hbm.1, bf16[100,1024]{1,0:T(8,128)(2,1)} %wo_hbm.1), custom_call_target="tpu_custom_call" | custom-call | tf_op jit(solution)/shard_map/crps_step/pallas_call | solution.py:582
  79.8 1.2 %hand_over.1 = (bf16[768,1024]{1,0:T(8,128)(2,1)}, f32[16,1024]{1,0:T(8,128)}) custom-call(bf16[768,1024]{1,0:T(8,128)(2,1)S(1)} %get-tuple-element.6.refs_0_, f32[16,1024]{1,0:T(8,128)S(1)} %get-tuple-element.7.refs_1_), custom_call_target="tpu_custom_call" | custom-call | tf_op jit(solution)/shard_map/hand_over/pallas_call | solution.py:518

commit v6 on v4

--- a/solution.py
+++ b/solution.py
@@ -43,6 +43,7 @@
     points, width = hid.shape
     half = width // 2
     quarter = half // 2
+    depth = width // n
     levels = truth.shape[0]
     count = finals.shape[0]
     chips = count // 2
@@ -128,8 +129,7 @@
             [(hid_hbm, hid), (gain_hbm, gain), (truth_hbm, truth), (lat_hbm, lat), (wo_hbm, wo_raw)]
         )
     ]
-    own_w.start()
-    for load in loads:
+    for load in loads[:2]:
         load.start()
     pl.semaphore_wait(barrier, nh * chips - chips + n - 1 + 2 + count - 1)
 
@@ -154,6 +154,9 @@
         loop(1, nh, lambda k: to_z(k, 0))
     else:
         from_end(spread_z)
+    own_w.start()
+    for load in loads[2:]:
+        load.start()
     loads[0].wait()
     loads[1].wait()
 
@@ -173,6 +176,14 @@
 
     span = min(LANES, points)
     turns = points // span
+
+    def rank(v, own):
+        near = jnp.where(v == own + 1 - 2 * (own % 2), 1, 2)
+        return jnp.where(v == own, 3, jnp.where(v == (own + 2) % n, 0, near))
+
+    ranks = [
+        [(core, rank(v, y)) for v in range(ny)], [(1 - core, rank(v, x)) for v in range(nx)]
+    ]
 
     def turn(i):
         cols = rows_at(i * span, span)
@@ -183,8 +194,9 @@
                     first = ((x_ * nh + h_) * ny + y_) * block
                     piece = turned[first:first + block, :]
                     to_x, to_y = (x_ * nh + h_) * block, (y_ * nh + h_) * block
-                    planes[0, y_, to_x:to_x + block, cols] = piece
-                    planes[1, x_, to_y:to_y + block, cols] = piece
+                    for (which, r), first in ((ranks[0][y_], to_x), (ranks[1][x_], to_y)):
+                        start = pl.multiple_of(r * depth + first, block)
+                        planes[which, pl.ds(start, block), cols] = piece
 
     loop(0, turns // 2, turn)
     own_w.wait()
@@ -218,7 +230,6 @@
         drain(own_group, a2_r.at[b - 1])
         to_second(b)
 
-    loop(1, n, pass_first)
 
     def pass_second(j):
         b = ordered(j)
@@ -229,7 +240,9 @@
         for i in range(2):
             to_partner(sides[i], b)
 
-    loop(0, n, pass_second)
+    pass_second(0)
+    loop(1, n, pass_first)
+    loop(1, n, pass_second)
 
     def pass_far(j):
         b = ordered(j)
@@ -249,9 +262,8 @@
         a = act[rows, cols]
         hidden_act[rows, cols] = (a * (0.5 * jnp.tanh(0.5 * a) + 0.5)).astype(bf16)
 
-    ahead = max(tiles - 1, 1)
-    loop(0, ahead, lambda t: project(rows_at(t * tile, tile), mine))
-    by_rows(0, ahead * tile, lambda rows: activate(rows, mine))
+    project(slice(0, points), mine)
+    by_rows(0, points, lambda rows: activate(rows, mine))
 
     drain(w_full.at[:, :, :, :, other], a4_r.at[0])
 
@@ -313,7 +325,7 @@
         s = 0.5 * jnp.tanh(0.5 * a) + 0.5
         act[rows, :] = s * (1.0 + a * (1.0 - s))
 
-    loop(0, ahead, forward)
+    loop(0, max(tiles - 1, 1), forward)
     truth_pad[...] = jnp.zeros_like(truth_pad)
     truth_pad[0:levels, :] = truth[...]
     truth_t[...] = truth_pad[...].T
@@ -322,10 +334,8 @@
     strip = lat.shape[1]
     for i in range(lat.shape[0]):
         area_t[i * strip:(i + 1) * strip, :] = jnp.broadcast_to(area[i:i + 1, :], (LANES, strip)).T
-    if ahead < tiles:
-        project(rows_at(ahead * tile, tile), mine)
-        tile_rows(ahead, lambda rows: activate(rows, mine))
-        forward(ahead)
+    if tiles > 1:
+        forward(tiles - 1)
 
     def reply_and_prepare(t):
         answer(t)
@@ -348,51 +358,44 @@
         grad_act = jnp.dot(grad_fields.astype(bf16), wo_pad[...], preferred_element_type=f32)
         gp[rows, :] = (grad_act * act[rows, :]).astype(bf16)
 
-    depth = width // n
-
-    def nth(i, own):
-        first = jnp.where(i == 0, (own + 2) % n, own + 1 - 2 * (own % 2))
-        return jnp.where(i < 2, first, jnp.where(i == 2, n - 1 - own, own))
-
-    def product(which, i):
-        plane, cols = (nth(i, p), mine) if which else (nth(i, q), other)
-        return jnp.dot(
-            planes[core if which else 1 - core, plane], gp[:, cols], preferred_element_type=f32
-        )
-
     loop(0, tiles, backward)
 
-    def other_plane(i):
-        part = product(0, i)
-        csend[i] = part.astype(bf16)
-        send(csend.at[i], crecv.at[i], c0_s.at[0], c0_r.at[i], partner)
-
-    loop(0, n, other_plane)
+    def product(which, pair, cols):
+        rows = rows_at(pair * 2 * depth, 2 * depth)
+        return jnp.dot(planes[which, rows, :], gp[:, cols], preferred_element_type=f32)
+
+    def other_pair(pair):
+        part = product(1, pair, other).astype(bf16)
+        for u in range(2):
+            i = 2 * pair + u
+            csend[i] = part[u * depth:(u + 1) * depth, :]
+            send(csend.at[i], crecv.at[i], c0_s.at[0], c0_r.at[i], partner)
+
+    loop(0, n // 2, other_pair)
 
     halves = [slice(0, quarter), slice(quarter, half)]
 
     def to_side(slot, target):
         send(send1.at[slot], recv1.at[slot], c1_s.at[0], c1_r.at[slot], p_peers[target])
 
-    def own_plane(i):
-        part = product(1, i)
-        drain(crecv.at[i], c0_r.at[i])
-        total = part + crecv[i].astype(f32)
-        sums[i] = total
-
-        @pl.when(i == 0)
-        def _():
-            for side in range(2):
-                send1[side] = total[:, halves[side]].astype(bf16)
-                to_side(side, side)
-
-        for side in range(2):
-            @pl.when(i == 1 + side)
-            def _():
-                send1[2 + side] = total[:, halves[side]].astype(bf16)
-                to_side(2 + side, side)
-
-    loop(0, n, own_plane)
+    def own_pair(pair):
+        part = product(0, pair, mine)
+        for u in range(2):
+            i = 2 * pair + u
+            drain(crecv.at[i], c0_r.at[i])
+            sums[i] = part[u * depth:(u + 1) * depth, :] + crecv[i].astype(f32)
+
+    def to_near(side):
+        send1[2 + side] = sums[1 + side, :, halves[side]].astype(bf16)
+        to_side(2 + side, side)
+
+    own_pair(0)
+    for side in range(2):
+        send1[side] = sums[0, :, halves[side]].astype(bf16)
+        to_side(side, side)
+    to_near(0)
+    own_pair(1)
+    to_near(1)
     for side in range(2):
         drain(recv1.at[side], c1_r.at[side])
         term = sums[2 - side, :, halves[side]] + recv1[side].astype(f32)
@@ -454,14 +457,14 @@
     for i in range(nh * chips - 1):
         total = total + recv3[i].astype(f32)
     factor = 1.0 / math.sqrt(count * points * nx * nh * ny)
-    finals[core * chips + low] = total * factor
+    finals[core * chips + low] = (total * factor).astype(bf16)
     own_final = finals.at[core * chips + low]
     loop(1, count, lambda k: send(own_final, own_final, c4_s.at[0], c4_r.at[0], m_peer(k)))
     by_rows(points // 2, points, hidden_grad)
     others = finals.at[pl.ds(0, count - 1)]
     drain(others, c4_r.at[0])
     for i in range(count):
-        gw_ref[:, i * strip:(i + 1) * strip] = finals[i]
+        gw_ref[:, i * strip:(i + 1) * strip] = finals[i].astype(f32)
 
     if chips == 1:
         drain(z_blocks, a1_s.at[0])
@@ -530,7 +533,7 @@
         vmem((levels, width), bf16),
         vmem((nx, nh, ny, block, width), bf16),
         vmem((points, width), bf16),
-        vmem((2, n, width // n, points), bf16),
+        vmem((2, width, points), bf16),
         vmem((points, LANES), f32),
         vmem((LANES, width), bf16),
         vmem((width, LANES), bf16),
@@ -554,7 +557,7 @@
         vmem((n - 1, nh * block, half), bf16),
         vmem((nh, chips, block, half // chips), bf16),
         vmem((nh * chips - 1, block, half // chips), bf16),
-        vmem((count, block, half // chips), f32),
+        vmem((count, block, half // chips), bf16),
         dma((6,)),
     ]
     for arrivals in (

time: 78 us -> 79.7 us (1.022)
  Pallas kernels: 77.2 us -> 79 us
    pallas_call x1, Pallas kernels: 76 us -> 77.7 us  [per_device(): pl.pallas_call(functools.partial(kernel, tile), out_shape=(vmem((points,...]
where the time goes in v6:
time: 79.7 us; the launch traced here: 79.6 us
  Pallas kernels  79 us (99%)
    pallas_call x1, Pallas kernels, per_device(): pl.pallas_call(functools.partial(kernel, tile), out_shape=(vmem((points,...  77.7 us

profile of v6, /device:TPU:1, one launch (start us, length us, event | category | flops | bytes accessed | tf_op | source)
XLA Modules:
  0.0 79.6 jit_solution(1256287090742352853)
XLA Ops:
  0.6 77.7 %crps_step.1 = (bf16[768,1024]{1,0:T(8,128)(2,1)S(1)}, f32[16,1024]{1,0:T(8,128)S(1)}) custom-call(bf16[768,1024]{1,0:T(8,128)(2,1)} %bitcast.4, f32[100,768]{1,0:T(8,128)} %truth_hbm.1, s32[6,128]{1,0:T(8,128)} %bitcast.5, f32[1,1024]{1,0:T(1,128)} %bitcast.6, bf16[16,1024]{1,0:T(8,128)(2,1)} %w_hbm.1, bf16[100,1024]{1,0:T(8,128)(2,1)} %wo_hbm.1), custom_call_target="tpu_custom_call" | custom-call | tf_op jit(solution)/shard_map/crps_step/pallas_call | solution.py:569
  78.4 1.2 %hand_over.1 = (bf16[768,1024]{1,0:T(8,128)(2,1)}, f32[16,1024]{1,0:T(8,128)}) custom-call(bf16[768,1024]{1,0:T(8,128)(2,1)S(1)} %get-tuple-element.6.refs_0_, f32[16,1024]{1,0:T(8,128)S(1)} %get-tuple-element.7.refs_1_), custom_call_target="tpu_custom_call" | custom-call | tf_op jit(solution)/shard_map/hand_over/pallas_call | solution.py:505

commit v7 on v6

--- a/solution.py
+++ b/solution.py
@@ -85,6 +85,10 @@
     far = (p + 2) % n
     p_peers = [at(v, q, h) for v in sides]
     partner = (member + 1 - 2 * core, space)
+    crossed = [(partner[0], peer[1]) for peer in p_peers]
+    crossing = [
+        (partner[0], at(p, v, h)[1]) for v in (q + 1 - 2 * (q % 2), n - 1 - q)
+    ]
 
     def send(src, dst, send_sem, recv_sem, target):
         pltpu.make_async_remote_copy(
@@ -118,7 +122,7 @@
 
     loop(chips, nh * chips, lambda i: greet(z_peer(i)))
     loop(1, n, lambda k: greet(q_peer(k)))
-    for peer in p_peers:
+    for peer in p_peers + crossing:
         greet(peer)
     loop(1, count, lambda k: greet(m_peer(k)))
 
@@ -131,7 +135,7 @@
     ]
     for load in loads[:2]:
         load.start()
-    pl.semaphore_wait(barrier, nh * chips - chips + n - 1 + 2 + count - 1)
+    pl.semaphore_wait(barrier, nh * chips - chips + n - 1 + 4 + count - 1)
 
     own_block = w_full.at[x, h, y, :, mine]
     def to_z(dh, l_):
@@ -237,6 +241,7 @@
             drain(own_group, a3_r.at[b, i])
             part = group(sides[i], b, quarters[i])
             send(part, part, a3_s.at[0], a3_r.at[b, 2 + i], p_peers[1 - i])
+            send(part, part, a3_s.at[0], a4_r.at[0], crossed[1 - i])
         for i in range(2):
             to_partner(sides[i], b)
 
@@ -248,7 +253,6 @@
         b = ordered(j)
         for i in range(2):
             drain(group(far, b, quarters[i]), a3_r.at[b, 2 + i])
-        to_partner(far, b)
 
     loop(0, n, pass_far)
 
@@ -471,8 +475,8 @@
     else:
         from_end(lambda toward, start: [drain(z_blocks, a1_s.at[0]) for _ in range(2)])
     drain(w_full.at[pl.ds(0, n - 1), :, 0, :, mine], a2_s.at[0])
-    drain(w_full.at[:, :, pl.ds(0, 3), :, mine], a3_s.at[0])
-    drain(w_full.at[:, :, :, :, mine], a4_s.at[0])
+    drain(w_full.at[:, :, :, :, mine], a3_s.at[0])
+    drain(w_full.at[:, :, pl.ds(0, 3), :, mine], a4_s.at[0])
     drain(coarse.at[pl.ds(0, points - points // count), :], b1_s.at[0])
     drain(coarse.at[pl.ds(0, points - points // count), :], b2_s.at[0])
     drain(csend, c0_s.at[0])

time: 79.7 us -> 79.5 us (level)
  no operation moved by 1% of the time
where the time goes in v7:
time: 79.5 us; the launch traced here: 79.3 us
  Pallas kernels  78.7 us (99%)
    pallas_call x1, Pallas kernels, per_device(): pl.pallas_call(functools.partial(kernel, tile), out_shape=(vmem((points,...  77.5 us

profile of v7, /device:TPU:1, one launch (start us, length us, event | category | flops | bytes accessed | tf_op | source)
XLA Modules:
  0.0 79.3 jit_solution(640970944431171829)
XLA Ops:
  0.6 77.5 %crps_step.1 = (bf16[768,1024]{1,0:T(8,128)(2,1)S(1)}, f32[16,1024]{1,0:T(8,128)S(1)}) custom-call(bf16[768,1024]{1,0:T(8,128)(2,1)} %bitcast.4, f32[100,768]{1,0:T(8,128)} %truth_hbm.1, s32[6,128]{1,0:T(8,128)} %bitcast.5, f32[1,1024]{1,0:T(1,128)} %bitcast.6, bf16[16,1024]{1,0:T(8,128)(2,1)} %w_hbm.1, bf16[100,1024]{1,0:T(8,128)(2,1)} %wo_hbm.1), custom_call_target="tpu_custom_call" | custom-call | tf_op jit(solution)/shard_map/crps_step/pallas_call | solution.py:573
  78.1 1.2 %hand_over.1 = (bf16[768,1024]{1,0:T(8,128)(2,1)}, f32[16,1024]{1,0:T(8,128)}) custom-call(bf16[768,1024]{1,0:T(8,128)(2,1)S(1)} %get-tuple-element.6.refs_0_, f32[16,1024]{1,0:T(8,128)S(1)} %get-tuple-element.7.refs_1_), custom_call_target="tpu_custom_call" | custom-call | tf_op jit(solution)/shard_map/hand_over/pallas_call | solution.py:509

commit v8 on v7

--- a/solution.py
+++ b/solution.py
@@ -266,8 +266,8 @@
         a = act[rows, cols]
         hidden_act[rows, cols] = (a * (0.5 * jnp.tanh(0.5 * a) + 0.5)).astype(bf16)
 
-    project(slice(0, points), mine)
-    by_rows(0, points, lambda rows: activate(rows, mine))
+    project(slice(0, tile), mine)
+    by_rows(0, tile, lambda rows: activate(rows, mine))
 
     drain(w_full.at[:, :, :, :, other], a4_r.at[0])
 
@@ -277,10 +277,15 @@
     def tile_rows(t, body):
         by_rows(0, tile, lambda rows: body(rows_at(t * tile + rows.start, 16)))
 
-    def forward(t):
+    def forward(t, whole=True):
         rows = rows_at(t * tile, tile)
-        project(rows, other)
-        tile_rows(t, lambda rows: activate(rows, other))
+        if whole:
+            act[rows, :] = jnp.dot(
+                normed[rows, :], w_full[...].reshape(width, width), preferred_element_type=f32
+            )
+        else:
+            project(rows, other)
+        tile_rows(t, lambda part: activate(part, slice(0, width) if whole else other))
         field = jnp.dot(hidden_act[rows, :], wo_t[...], preferred_element_type=f32)
         fields[rows, :] = field
         coarse[rows, :] = field.astype(bf16)
@@ -329,7 +334,8 @@
         s = 0.5 * jnp.tanh(0.5 * a) + 0.5
         act[rows, :] = s * (1.0 + a * (1.0 - s))
 
-    loop(0, max(tiles - 1, 1), forward)
+    forward(0, whole=False)
+    loop(1, tiles - 1, forward)
     truth_pad[...] = jnp.zeros_like(truth_pad)
     truth_pad[0:levels, :] = truth[...]
     truth_t[...] = truth_pad[...].T

time: 79.5 us -> 79 us (level)
  no operation moved by 1% of the time
where the time goes in v8:
time: 79 us; the launch traced here: 78.9 us
  Pallas kernels  78.2 us (99%)
    pallas_call x1, Pallas kernels, per_device(): pl.pallas_call(functools.partial(kernel, tile), out_shape=(vmem((points,...  77 us

profile of v8, /device:TPU:1, one launch (start us, length us, event | category | flops | bytes accessed | tf_op | source)
XLA Modules:
  0.0 78.9 jit_solution(8344484545153387168)
XLA Ops:
  0.6 77.0 %crps_step.1 = (bf16[768,1024]{1,0:T(8,128)(2,1)S(1)}, f32[16,1024]{1,0:T(8,128)S(1)}) custom-call(bf16[768,1024]{1,0:T(8,128)(2,1)} %bitcast.4, f32[100,768]{1,0:T(8,128)} %truth_hbm.1, s32[6,128]{1,0:T(8,128)} %bitcast.5, f32[1,1024]{1,0:T(1,128)} %bitcast.6, bf16[16,1024]{1,0:T(8,128)(2,1)} %w_hbm.1, bf16[100,1024]{1,0:T(8,128)(2,1)} %wo_hbm.1), custom_call_target="tpu_custom_call" | custom-call | tf_op jit(solution)/shard_map/crps_step/pallas_call | solution.py:579
  77.7 1.2 %hand_over.1 = (bf16[768,1024]{1,0:T(8,128)(2,1)}, f32[16,1024]{1,0:T(8,128)}) custom-call(bf16[768,1024]{1,0:T(8,128)(2,1)S(1)} %get-tuple-element.6.refs_0_, f32[16,1024]{1,0:T(8,128)S(1)} %get-tuple-element.7.refs_1_), custom_call_target="tpu_custom_call" | custom-call | tf_op jit(solution)/shard_map/hand_over/pallas_call | solution.py:515

commit v9 on v8

--- a/solution.py
+++ b/solution.py
@@ -202,7 +202,7 @@
                         start = pl.multiple_of(r * depth + first, block)
                         planes[which, pl.ds(start, block), cols] = piece
 
-    loop(0, turns // 2, turn)
+    loop(0, turns, turn)
     own_w.wait()
     z_blocks = w_full.at[0, 0, pl.ds(0, nh - 1), :, mine]
     drain(z_blocks, a1_r.at[0])
@@ -264,7 +264,9 @@
 
     def activate(rows, cols):
         a = act[rows, cols]
-        hidden_act[rows, cols] = (a * (0.5 * jnp.tanh(0.5 * a) + 0.5)).astype(bf16)
+        s = 0.5 * jnp.tanh(0.5 * a) + 0.5
+        hidden_act[rows, cols] = (a * s).astype(bf16)
+        act[rows, cols] = s * (1.0 + a * (1.0 - s))
 
     project(slice(0, tile), mine)
     by_rows(0, tile, lambda rows: activate(rows, mine))
@@ -329,11 +331,6 @@
         pairs[share_of(t, member), :] = answers[t, member]
 
 
-    def differentiate(rows):
-        a = act[rows, :]
-        s = 0.5 * jnp.tanh(0.5 * a) + 0.5
-        act[rows, :] = s * (1.0 + a * (1.0 - s))
-
     forward(0, whole=False)
     loop(1, tiles - 1, forward)
     truth_pad[...] = jnp.zeros_like(truth_pad)
@@ -347,13 +344,7 @@
     if tiles > 1:
         forward(tiles - 1)
 
-    def reply_and_prepare(t):
-        answer(t)
-        tile_rows(t, differentiate)
-        left = turns - turns // 2
-        loop(turns // 2 + t * left // tiles, turns // 2 + (t + 1) * left // tiles, turn)
-
-    loop(0, tiles, reply_and_prepare)
+    loop(0, tiles, answer)
 
     fair = (1.0 - (1.0 - ALPHA) / count) / (count * (count - 1))
 

time: 79 us -> 79.5 us (level)
  no operation moved by 1% of the time
where the time goes in v9:
time: 79.5 us; the launch traced here: 79.4 us
  Pallas kernels  78.8 us (99%)
    pallas_call x1, Pallas kernels, per_device(): pl.pallas_call(functools.partial(kernel, tile), out_shape=(vmem((points,...  77.5 us

profile of v9, /device:TPU:1, one launch (start us, length us, event | category | flops | bytes accessed | tf_op | source)
XLA Modules:
  0.0 79.4 jit_solution(6927696959246605827)
XLA Ops:
  0.6 77.5 %crps_step.1 = (bf16[768,1024]{1,0:T(8,128)(2,1)S(1)}, f32[16,1024]{1,0:T(8,128)S(1)}) custom-call(bf16[768,1024]{1,0:T(8,128)(2,1)} %bitcast.4, f32[100,768]{1,0:T(8,128)} %truth_hbm.1, s32[6,128]{1,0:T(8,128)} %bitcast.5, f32[1,1024]{1,0:T(1,128)} %bitcast.6, bf16[16,1024]{1,0:T(8,128)(2,1)} %w_hbm.1, bf16[100,1024]{1,0:T(8,128)(2,1)} %wo_hbm.1), custom_call_target="tpu_custom_call" | custom-call | tf_op jit(solution)/shard_map/crps_step/pallas_call | solution.py:570
  78.2 1.2 %hand_over.1 = (bf16[768,1024]{1,0:T(8,128)(2,1)}, f32[16,1024]{1,0:T(8,128)}) custom-call(bf16[768,1024]{1,0:T(8,128)(2,1)S(1)} %get-tuple-element.6.refs_0_, f32[16,1024]{1,0:T(8,128)S(1)} %get-tuple-element.7.refs_1_), custom_call_target="tpu_custom_call" | custom-call | tf_op jit(solution)/shard_map/hand_over/pallas_call | solution.py:506

commit v10 on v8

--- a/solution.py
+++ b/solution.py
@@ -16,7 +16,7 @@
 
 GRID = (4, 4, 4)
 LANES = 128
-TILE = 256
+TILE = 384
 MESH = pl.DeviceIdType.MESH
 
 

time: 79 us -> 79.9 us (1.011)
  Pallas kernels: 78.2 us -> 79.1 us
    pallas_call x1, Pallas kernels: 77 us -> 77.9 us  [per_device(): pl.pallas_call(functools.partial(kernel, tile), out_shape=(vmem((points,...]
where the time goes in v10:
time: 79.9 us; the launch traced here: 79.8 us
  Pallas kernels  79.1 us (99%)
    pallas_call x1, Pallas kernels, per_device(): pl.pallas_call(functools.partial(kernel, tile), out_shape=(vmem((points,...  77.9 us

profile of v10, /device:TPU:1, one launch (start us, length us, event | category | flops | bytes accessed | tf_op | source)
XLA Modules:
  0.0 79.8 jit_solution(16508368461452566538)
XLA Ops:
  0.6 77.9 %crps_step.1 = (bf16[768,1024]{1,0:T(8,128)(2,1)S(1)}, f32[16,1024]{1,0:T(8,128)S(1)}) custom-call(bf16[768,1024]{1,0:T(8,128)(2,1)} %bitcast.4, f32[100,768]{1,0:T(8,128)} %truth_hbm.1, s32[6,128]{1,0:T(8,128)} %bitcast.5, f32[1,1024]{1,0:T(1,128)} %bitcast.6, bf16[16,1024]{1,0:T(8,128)(2,1)} %w_hbm.1, bf16[100,1024]{1,0:T(8,128)(2,1)} %wo_hbm.1), custom_call_target="tpu_custom_call" | custom-call | tf_op jit(solution)/shard_map/crps_step/pallas_call | solution.py:579
  78.5 1.2 %hand_over.1 = (bf16[768,1024]{1,0:T(8,128)(2,1)}, f32[16,1024]{1,0:T(8,128)}) custom-call(bf16[768,1024]{1,0:T(8,128)(2,1)S(1)} %get-tuple-element.6.refs_0_, f32[16,1024]{1,0:T(8,128)S(1)} %get-tuple-element.7.refs_1_), custom_call_target="tpu_custom_call" | custom-call | tf_op jit(solution)/shard_map/hand_over/pallas_call | solution.py:515
